TPU v7x, 256 devices: a whole 4x4x8 slice. The times are simulated.
256 devices in a mesh: gy: 32 (over y, z), gz: 8 (over x, core).
Axes of the slice: x: 4, y: 4, z: 8, core: 2. Of those that a mesh axis runs over, the one named last changes fastest.
Arguments:
- fields: float32 [2048, 4, 256, 128], P('gy', None, 'gz'), may hold values from -6 to 6
- kappa: float32 [2048, 256, 128], P('gy', 'gz'), may hold values from 0.02 to 0.16
- forward_mult: float32 [2048, 4], P('gy'), may hold values from 0.995 to 0.999
- pivot_inv: float32 [2048, 4], P('gy'), may hold values from 0.0001 to 0.001
- backward_mult: float32 [2048, 4], P('gy'), may hold values from 0.995 to 0.999
Outputs:
- solved: float32 [2048, 4, 256, 128], P('gy', None, 'gz')
All inputs are finite; a program needn't handle non-finite values.
Results may differ from a plain program's by a relative error of at most 0.00021.
Values sent between devices are 32-bit elements; how exact they have to be, the bound alone decides.
No kernel may reach another device: no remote copies, remote signals or barrier semaphores. Data moves between devices by JAX's collectives and lax.ppermute only.
A program may use at most 128 MiB of HBM per device.

v0:
```python
import jax
import jax.numpy as jnp
from jax import lax
from jax.sharding import PartitionSpec as P


def with_halo(cells, sides, width, closed):
    for axis, dim in sides:
        count = lax.axis_size(axis)
        ends = count if closed else count - 1
        head = lax.slice_in_dim(cells, 0, width, axis=dim)
        tail = lax.slice_in_dim(cells, cells.shape[dim] - width, cells.shape[dim], axis=dim)
        cells = jnp.concatenate(
            [
                lax.ppermute(tail, axis, [(i, (i + 1) % count) for i in range(ends)]),
                cells,
                lax.ppermute(head, axis, [((i + 1) % count, i) for i in range(ends)]),
            ],
            axis=dim,
        )
    return cells


def entering_2(part, axis, combine, identity, reverse):
    count = lax.axis_size(axis)
    place = lax.axis_index(axis)
    ahead = count - 1 - place if reverse else place
    gathered = jax.tree.map(lambda a: lax.all_gather(a, axis), part)
    state = jax.tree.map(lambda a, e: jnp.zeros_like(a) + jnp.asarray(e, a.dtype), part, identity)

    def one(lap, state):
        source = count - 1 - lap if reverse else lap
        return combine(
            state, jax.tree.map(lambda a: lax.dynamic_index_in_dim(a, source, 0, False), gathered)
        )

    return lax.fori_loop(0, ahead, one, state)


def combine(earlier, later):
    return (earlier[0] * later[0], earlier[1] * later[0] + later[1])


def local_rows(values, factors, reverse):
    logs = jnp.log(factors)
    totals = jnp.cumsum(logs, axis=0)
    count = values.shape[0]
    row_ids = lax.broadcasted_iota(jnp.int32, (count, count), 0)
    col_ids = lax.broadcasted_iota(jnp.int32, (count, count), 1)
    if reverse:
        before = totals - logs
        exponent = before[None, :, :] - before[:, None, :]
        keep = col_ids >= row_ids
    else:
        exponent = totals[:, None, :] - totals[None, :, :]
        keep = col_ids <= row_ids
    keep = keep[:, :, None]
    weights = jnp.where(keep, jnp.exp(jnp.where(keep, exponent, 0.0)), 0.0)
    return jnp.einsum("ijf,jfzx->ifzx", weights, values, precision=lax.Precision.HIGHEST)


def on_device(fields, kappa, forward_mult, pivot_inv, backward_mult):
    wall_wide = with_halo(fields, (("gy", 0),), 1, False)
    wall_sum = wall_wide[2:] + wall_wide[:-2]
    span_wide = with_halo(fields, (("gz", 2),), 1, True)
    span_sum = span_wide[:, :, 2:] + span_wide[:, :, :-2]
    stream_sum = jnp.roll(fields, 1, 3) + jnp.roll(fields, -1, 3)
    beside_all = wall_sum + span_sum + stream_sum
    right = fields + kappa[:, None] * (beside_all - 6.0 * fields)
    lifted = right[:, 2] + 0.5 * fields[:, 0]
    right = jnp.concatenate([right[:, :2], lifted[:, None], right[:, 3:]], axis=1)
    forward_zero = local_rows(right, forward_mult, False)
    forward_prod = jnp.cumprod(forward_mult, axis=0)
    forward_factor = forward_prod[-1][:, None, None]
    forward_value = forward_zero[-1]
    prefix = entering_2(
        (forward_factor, forward_value),
        "gy",
        combine,
        (jnp.ones_like(forward_factor), jnp.zeros_like(forward_value)),
        False,
    )
    entering = prefix[1]
    swept = forward_zero + forward_prod[:, :, None, None] * entering[None]
    scaled = pivot_inv[:, :, None, None] * swept
    backward_zero = local_rows(scaled, backward_mult, True)
    backward_prod = jnp.cumprod(backward_mult[::-1], axis=0)[::-1]
    backward_factor = backward_prod[0][:, None, None]
    backward_value = backward_zero[0]
    suffix = entering_2(
        (backward_factor, backward_value),
        "gy",
        combine,
        (jnp.ones_like(backward_factor), jnp.zeros_like(backward_value)),
        True,
    )
    arriving = suffix[1]
    return backward_zero + backward_prod[:, :, None, None] * arriving[None]


def solution(mesh):
    placed = (
        P("gy", None, "gz", None),
        P("gy", "gz", None),
        P("gy", None),
        P("gy", None),
        P("gy", None),
    )
    return jax.shard_map(
        on_device, mesh=mesh, in_specs=placed, out_specs=P("gy", None, "gz", None), check_vma=False
    )
```

profile of v0, /device:TPU:2, one launch (start us, length us, event | category | flops | bytes accessed | tf_op | source)
XLA Modules:
  0.0 290.4 jit_solution(12792023846403344505)
XLA Ops:
  6.5 4.6 %copy.54 = f32[64,4,32,128]{3,0,2,1:T(8,128)S(1)} copy(f32[64,4,32,128]{3,2,1,0:T(8,128)} %param.9) | data formatting | bytes 8388608 | tf_op args[0]
  11.2 0.5 collective-permute-start.3
  11.7 1.0 fusion.50
  12.7 1.3 collective-permute-start
  14.0 4.7 %collective-permute-start.1 = (f32[1,4,32,128]{3,0,2,1:T(1,128)S(1)}, f32[1,4,32,128]{3,0,2,1:T(1,128)S(1)}, u32[]{:S(2)}, u32[]{:S(2)}) collective-permute-start(f32[1,4,32,128]{3,0,2,1:T(1,128)S(1)} %bitcast.46), channel_id=1, source_target_pairs={{0,8},{8,16},{16,24},{24,32},{32,40},{40,48},{48,56},{56,64},{64,7... | collective-permute-start | bytes 196616 | tf_op jit(solution)/shard_map/ppermute | solution.py:15
  18.8 4.6 %fusion.48 = (f32[64,4,32,127]{3,0,2,1:T(8,128)}, f32[64,4,32,127]{3,0,2,1:T(8,128)}) fusion(f32[64,4,32,128]{3,0,2,1:T(8,128)S(1)} %copy.54), kind=kLoop, calls=%fused_computation.59 | loop fusion | bytes 16646144 | tf_op jit(solution)/shard_map/jit(_roll_static)/slice | solution.py:67
  23.4 4.6 %fusion.49 = (f32[64,4,32,1]{3,0,2,1:T(8,128)}, f32[64,4,32,1]{3,0,2,1:T(8,128)}) fusion(f32[64,4,32,128]{3,0,2,1:T(8,128)S(1)} %copy.54), kind=kLoop, calls=%fused_computation.60 | loop fusion | bytes 131072 | tf_op jit(solution)/shard_map/jit(_roll_static)/slice | solution.py:67
  28.0 0.6 copy.40
  28.6 0.1 copy.56
  28.7 0.1 reduce_window_sum.17
  29.0 15.1 %fusion.5 = f32[64,4,32,128]{3,0,2,1:T(8,128)S(1)} fusion(f32[64,4,32,128]{3,0,2,1:T(8,128)} %copy-done, f32[64,4,1,128]{3,0,2,1:T(8,128)S(1)} %collective-permute-done.3, f32[64,4,1,128]{3,0,2,1:T(8,128)S(1)} %collective-permute-done.2, f32[1,4,32,128]{3,0,2,1:T(1,128)S(1)} %collective-permute-done.1, f32[1,4,32,128]{3,0,2,1:T(1,128)S(1)} %collective-permute-done, ...), kind=kLoop, calls=%fused_computation.10 | loop fusion | flops 15728640 | bytes 18219008 | tf_op jit(solution)/shard_map/add | solution.py:69
  44.1 1.5 fusion.26
  45.6 0.2 slice.95
  45.9 4.0 %fusion.17 = f32[64,4,32,128]{3,0,2,1:T(8,128)S(1)} fusion(f32[64,1,32,128]{3,0,2,1:T(8,128)S(1)} %get-tuple-element.176, f32[64,1,32,128]{3,0,2,1:T(8,128)S(1)} %get-tuple-element.175, f32[64,2,32,128]{3,0,2,1:T(8,128)S(1)} %slice.95, f32[64,4]{0,1:T(4,128)S(1)} %copy.57, pred[64,64]{1,0:T(8,128)(4,1)S(1)} %iota_compare_fusion.1), kind=kOutput, calls=%fused_computation.27 | convolution fusion | flops 807452672 | bytes 8393728 | tf_op jit(solution)/shard_map/ijf,jfzx->ifzx/dot_general | solution.py:59
  49.9 2.0 copy-done.1
  51.9 0.7 slice.100
  52.7 0.1 copy.59
  52.8 0.1 copy.64
  52.9 0.1 reduce_window_sum.18
  53.1 0.1 reduce_window.14
  53.2 43.2 %all-gather.2 = f32[32,1,4]{2,1,0:T(1,128)S(1)} all-gather(f32[1,1,4]{2,1,0:T(1,128)S(1)} %slice_bitcast_fusion.1), channel_id=2, replica_groups=mesh['gy'=32,'gz'=8] {'gy'}, dimensions={0}, use_global_device_ids=true | all-gather | bytes 528 | tf_op jit(solution)/shard_map/all_gather | solution.py:28
  96.5 38.9 %all-gather.7.cloned.1.call-done = f32[32,4,32,128]{3,2,1,0:T(8,128)} async-done(((f32[1,4,32,128]{3,2,1,0:T(8,128)}), f32[32,4,32,128]{3,2,1,0:T(8,128)}) %all-gather.7.cloned.1.call-update) | async-done | bytes 2097168 | tf_op jit(solution)/shard_map/all_gather | solution.py:28
  135.4 6.3 %fusion.20 = f32[64,4,32,128]{3,0,2,1:T(8,128)S(1)} fusion(f32[64,4,32,128]{3,0,2,1:T(8,128)} %copy-done.1, f32[4,32,128]{2,1,0:T(8,128)S(1)} %get-tuple-element.133, f32[64,4]{0,1:T(4,128)S(1)} %copy.60, f32[64,4]{0,1:T(4,128)S(1)} %copy-done.6, f32[64,4]{0,1:T(4,128)S(1)} %copy.66, pred[64,64]{1,0:T(8,128)(4,1)S(1)} %iota_compare_fusion), kind=kOutput, calls=%fused_computation.28 | convolution fusion | flops 808501248 | bytes 8461312 | tf_op jit(solution)/shard_map/ijf,jfzx->ifzx/dot_general | solution.py:59
  141.8 2.0 copy-done.2
  143.8 0.7 slice.102
  144.5 0.1 rev.6
  144.6 0.1 copy.68
  144.7 0.1 reduce_window.15
  144.9 63.3 %all-gather.3 = f32[32,1,4]{2,1,0:T(1,128)S(1)} all-gather(f32[1,1,4]{2,1,0:T(1,128)S(1)} %slice_bitcast_fusion), channel_id=3, replica_groups=mesh['gy'=32,'gz'=8] {'gy'}, dimensions={0}, use_global_device_ids=true | all-gather | bytes 528 | tf_op jit(solution)/shard_map/all_gather | solution.py:28
  208.1 39.0 %all-gather.9.cloned.1.call-done = f32[32,4,32,128]{3,2,1,0:T(8,128)} async-done(((f32[1,4,32,128]{3,2,1,0:T(8,128)}), f32[32,4,32,128]{3,2,1,0:T(8,128)}) %all-gather.9.cloned.1.call-update) | async-done | bytes 2097168 | tf_op jit(solution)/shard_map/all_gather | solution.py:28
  247.1 28.7 %while.27 = (s32[]{:T(128)}, f32[4,32,128]{2,1,0:T(8,128)S(1)}, s32[]{:T(128)}, f32[32,4,1,1]{1,3,2,0:T(1,128)S(1)}, f32[32,4,32,128]{3,2,1,0:T(8,128)}, /*index=5*/s32[]{:T(128)}, s32[]{:T(128)}, s32[]{:T(128)}, s32[]{:T(128)}) while((s32[]{:T(128)}, f32[4,32,128]{2,1,0:T(8,128)S(1)}, s32[]{:T(128)}, f32[32,4,1,1]{1,3,2,0:T(1,128)S(1)}, ...), condition=%wide.region_7.8_spmd, body=%wide.region_6.7_spmd.sunk | while | flops 32774 | bytes 196803 | solution.py:37
  247.1 0.9 bitcast_add_fusion.5
  248.1 0.9 bitcast_add_fusion.5
  249.0 0.9 bitcast_add_fusion.5
  249.9 0.9 bitcast_add_fusion.5
  250.8 0.9 bitcast_add_fusion.5
  251.8 0.9 bitcast_add_fusion.5
  252.7 0.9 bitcast_add_fusion.5
  253.6 0.9 bitcast_add_fusion.5
  254.5 0.9 bitcast_add_fusion.5
  255.5 0.9 bitcast_add_fusion.5
  256.4 0.9 bitcast_add_fusion.5
  257.3 0.9 bitcast_add_fusion.5
  258.3 0.9 bitcast_add_fusion.5
  259.2 0.9 bitcast_add_fusion.5
  260.1 0.9 bitcast_add_fusion.5
  261.0 0.9 bitcast_add_fusion.5
  262.0 0.9 bitcast_add_fusion.5
  262.9 0.9 bitcast_add_fusion.5
  263.8 0.9 bitcast_add_fusion.5
  264.7 0.9 bitcast_add_fusion.5
  265.7 0.9 bitcast_add_fusion.5
  266.6 0.9 bitcast_add_fusion.5
  267.5 0.9 bitcast_add_fusion.5
  268.5 0.9 bitcast_add_fusion.5
  269.4 0.9 bitcast_add_fusion.5
  270.3 0.9 bitcast_add_fusion.5
  271.2 0.9 bitcast_add_fusion.5
  272.2 0.9 bitcast_add_fusion.5
  273.1 0.9 bitcast_add_fusion.5
  274.0 0.9 bitcast_add_fusion.5
  274.9 0.9 bitcast_add_fusion.5
  275.9 3.2 %multiply_add_fusion = f32[64,4,32,128]{3,0,2,1:T(8,128)S(1)} fusion(f32[64,4,32,128]{3,0,2,1:T(8,128)} %copy-done.2, f32[4,32,128]{2,1,0:T(8,128)S(1)} %get-tuple-element.134, f32[64,4]{0,1:T(4,128)S(1)} %copy.69), kind=kLoop, calls=%fused_computation.22 | loop fusion | flops 2097152 | bytes 8455168 | tf_op jit(solution)/shard_map/add | solution.py:98
  279.1 4.4 %copy.73 = f32[64,4,32,128]{3,2,1,0:T(8,128)} copy(f32[64,4,32,128]{3,0,2,1:T(8,128)S(1)} %multiply_add_fusion) | data formatting | bytes 8388608 | tf_op jit(solution)/shard_map/add | solution.py:98
  (68 shorter events, 0.6 us)
Async XLA Ops:
  6.5 128.9 %all-gather.7.cloned.1.call-start = ((), (), s32[]{:S(2)}) async-start(), calls=%async_computation | async-start | bytes 2162688 | tf_op jit(solution)/shard_map/all_gather | solution.py:28
  11.2 12.2 %copy-start = (f32[64,4,32,128]{3,0,2,1:T(8,128)}, f32[64,4,32,128]{3,0,2,1:T(8,128)S(1)}, u32[]{:S(2)}) copy-start(f32[64,4,32,128]{3,0,2,1:T(8,128)S(1)} %copy.54) | copy-start | bytes 12582916
  11.2 17.8 %collective-permute-start.2 = (f32[64,4,1,128]{3,0,2,1:T(8,128)S(1)}, f32[64,4,1,128]{3,0,2,1:T(8,128)S(1)}, u32[]{:S(2)}, u32[]{:S(2)}) collective-permute-start(f32[64,4,1,128]{3,0,2,1:T(8,128)S(1)} %get-tuple-element.183), channel_id=1, source_target_pairs={{1,0},{2,1},{3,2},{4,3},{5,4},{6,5},{7,6},{0,7},{9,8},{10,9},{11,1... | collective-permute-start | bytes 393224 | tf_op jit(solution)/shard_map/ppermute | solution.py:17
  11.2 17.7 %collective-permute-start.3 = (f32[64,4,1,128]{3,0,2,1:T(8,128)S(1)}, f32[64,4,1,128]{3,0,2,1:T(8,128)S(1)}, u32[]{:S(2)}, u32[]{:S(2)}) collective-permute-start(f32[64,4,1,128]{3,0,2,1:T(8,128)S(1)} %get-tuple-element.184), channel_id=1, source_target_pairs={{0,1},{1,2},{2,3},{3,4},{4,5},{5,6},{6,7},{7,0},{8,9},{9,10},{10,1... | collective-permute-start | bytes 393224 | tf_op jit(solution)/shard_map/ppermute | solution.py:15
  12.7 16.2 %collective-permute-start = (f32[1,4,32,128]{3,0,2,1:T(1,128)S(1)}, f32[1,4,32,128]{3,0,2,1:T(1,128)S(1)}, u32[]{:S(2)}, u32[]{:S(2)}) collective-permute-start(f32[1,4,32,128]{3,0,2,1:T(1,128)S(1)} %bitcast.47), channel_id=1, source_target_pairs={{8,0},{16,8},{24,16},{32,24},{40,32},{48,40},{56,48},{64,56},{72,6... | collective-permute-start | bytes 196616 | tf_op jit(solution)/shard_map/ppermute | solution.py:17
  14.0 14.9 %collective-permute-start.1 = (f32[1,4,32,128]{3,0,2,1:T(1,128)S(1)}, f32[1,4,32,128]{3,0,2,1:T(1,128)S(1)}, u32[]{:S(2)}, u32[]{:S(2)}) collective-permute-start(f32[1,4,32,128]{3,0,2,1:T(1,128)S(1)} %bitcast.46), channel_id=1, source_target_pairs={{0,8},{8,16},{16,24},{24,32},{32,40},{40,48},{48,56},{56,64},{64,7... | collective-permute-start | bytes 196616 | tf_op jit(solution)/shard_map/ppermute | solution.py:15
  23.4 4.6 %copy-start.3 = (f32[64,32,128]{2,1,0:T(8,128)S(1)}, f32[64,32,128]{2,1,0:T(8,128)}, u32[]{:S(2)}) copy-start(f32[64,32,128]{2,1,0:T(8,128)} %param.10) | copy-start | bytes 3145732
  23.4 5.2 %copy-start.4 = (f32[64,4]{0,1:T(4,128)S(1)}, f32[64,4]{0,1:T(4,128)}, u32[]{:S(2)}) copy-start(f32[64,4]{0,1:T(4,128)} %param.11) | copy-start | bytes 3076
  45.8 6.9 %copy-start.5 = (f32[64,4]{0,1:T(4,128)S(1)}, f32[64,4]{0,1:T(4,128)}, u32[]{:S(2)}) copy-start(f32[64,4]{0,1:T(4,128)} %param.13) | copy-start | bytes 3076
  45.8 89.5 %copy-start.6 = (f32[64,4]{0,1:T(4,128)S(1)}, f32[64,4]{0,1:T(4,128)}, u32[]{:S(2)}) copy-start(f32[64,4]{0,1:T(4,128)} %param.12) | copy-start | bytes 3076
  49.9 2.0 copy-start.1
  52.6 194.5 %all-gather.9.cloned.1.call-start = ((), (), s32[]{:S(2)}) async-start(), calls=%async_computation.1 | async-start | bytes 2162688 | tf_op jit(solution)/shard_map/all_gather | solution.py:28
  141.8 2.0 copy-start.2
Sparse Core Ops, SparseCore 0:
  52.7 82.5 all-gather.6
  144.6 102.4 all-gather.8
where the time goes:
time: 292 us; the launch traced here: 290 us
  blocking collectives  106 us (36%)
  waiting for transfers between devices  77.9 us (27%)
  other arithmetic  48.8 us (17%)
  local copies, waits for them, and re-layouts  26.5 us (9%)
  between operations  13.6 us (5%)
  matrix products  10.4 us (4%)
  starting transfers between devices  6.58 us (2%)
    all_gather x2, blocking collectives, entering_2(): gathered = jax.tree.map(lambda a: lax.all_gather(a, axis), part)  106 us
    all_gather x2, waiting for transfers between devices, entering_2(): gathered = jax.tree.map(lambda a: lax.all_gather(a, axis), part)  77.9 us
    add x31, other arithmetic, combine(): return (earlier[0] * later[0], earlier[1] * later[0] + later[1])  28.6 us
    add x1, other arithmetic, on_device(): right = fields + kappa[:, None] * (beside_all - 6.0 * fields)  15.1 us
    dot_general x2, matrix products, local_rows(): jnp.einsum('ijf,jfzx->ifzx', weights, values, precision=lax.Precision.HIG...  10.4 us
    unnamed x19, local copies, waits for them, and re-layouts  9.37 us
    slice x2, local copies, waits for them, and re-layouts, on_device(): stream_sum = jnp.roll(fields, 1, 3) + jnp.roll(fields, -1, 3)  9.21 us
  transfers between devices with their start and end apart: 6, of which 2 were waited for; matrix products, arithmetic and copies ran while one was open for 4% of the time, Pallas kernels for 0%

commit v1 on v0

v1 whole, which is shorter than its diff:
```python
import jax
import jax.numpy as jnp
from jax import lax
from jax.experimental import pallas as pl
from jax.experimental.pallas import tpu as pltpu
from jax.sharding import Mesh
from jax.sharding import PartitionSpec as P

GY = ("y", "z")
GZ = ("x", "c")
FIELDS = 4
TILE = 8
STEP = 8
ROWS = 2 * FIELDS + 1
COEF_LANES = 8

VMEM = pl.BlockSpec(memory_space=pltpu.VMEM)
SMEM = pl.BlockSpec(memory_space=pltpu.SMEM)
HBM = pl.BlockSpec(memory_space=pltpu.HBM)
f32 = jnp.float32


def row_of(shape):
    return lax.broadcasted_iota(jnp.int32, shape, 0)


def lane_of(shape):
    return lax.broadcasted_iota(jnp.int32, shape, 1)


def collect(side, fields, inner, outer, near, far, sems):
    rows, _, span, _ = fields.shape
    z_near = jnp.where(side[0] == 0, span - 1, 0)
    j_near = jnp.where(side[1] == 0, rows - 1, 0)
    copies = [
        pltpu.make_async_copy(fields.at[:, :, pl.ds(span - 1 - z_near, 1)], outer, sems.at[0]),
        pltpu.make_async_copy(fields.at[:, :, pl.ds(z_near, 1)], inner, sems.at[1]),
        pltpu.make_async_copy(fields.at[j_near], near, sems.at[2]),
        pltpu.make_async_copy(fields.at[rows - 1 - j_near], far, sems.at[3]),
    ]
    for copy in copies:
        copy.start()
    for copy in copies:
        copy.wait()


def interior(fields, kappa, fwd, piv, bwd, base, last, first, rim, walls, held, weight, sweep, sems):
    rows, _, span, lanes = fields.shape
    tiles = span // TILE
    tile = (TILE, lanes)
    sub = row_of(tile)
    zero = jnp.zeros(tile, f32)
    chunks = rows // STEP

    def load(c):
        here = pl.ds(c * STEP, STEP)
        return (
            pltpu.make_async_copy(fields.at[here], held.at[pl.ds(1 + c * STEP, STEP)], sems.at[0, c]),
            pltpu.make_async_copy(kappa.at[here], weight.at[here], sems.at[1, c]),
        )

    for c in range(chunks):
        for copy in load(c):
            copy.start()
    for f in range(FIELDS):
        for v in range(tiles):
            held[0, f, pl.ds(v * TILE, TILE)] = zero
            held[rows + 1, f, pl.ds(v * TILE, TILE)] = zero
    for copy in load(0):
        copy.wait()

    def forward(c, carry):
        @pl.when(c < chunks - 1)
        def _():
            for copy in load(c + 1):
                copy.wait()

        state = list(carry)
        for i in range(STEP):
            j = c * STEP + i
            rim[j] = jnp.where(sub < FIELDS, weight[j, pl.ds(0, 1)], weight[j, pl.ds(span - 1, 1)])
        for f in range(FIELDS):
            for v in range(tiles):
                here = pl.ds(v * TILE, TILE)
                k = f * tiles + v
                under = held[c * STEP, f, here]
                x = held[c * STEP + 1, f, here]
                for i in range(STEP):
                    j = c * STEP + i
                    over = held[j + 2, f, here]
                    if v == 0:
                        left = jnp.where(sub == 0, 0.0, pltpu.roll(x, 1, 0))
                    else:
                        left = held[j + 1, f, pl.ds(v * TILE - 1, TILE)]
                    if v == tiles - 1:
                        right = jnp.where(sub == TILE - 1, 0.0, pltpu.roll(x, TILE - 1, 0))
                    else:
                        right = held[j + 1, f, pl.ds(v * TILE + 1, TILE)]
                    around = (left + right) + (pltpu.roll(x, 1, 1) + pltpu.roll(x, lanes - 1, 1))
                    around = around + (under + over)
                    new = x + weight[j, here] * (around - 6.0 * x)
                    if f == 2:
                        new = new + 0.5 * held[j + 1, 0, here]
                    state[k] = new + fwd[f, j] * state[k]
                    sweep[j, f, here] = state[k]
                    under, x = x, over
        return tuple(state)

    start = (zero,) * (FIELDS * tiles)
    state = lax.fori_loop(0, chunks, forward, start)
    for f in range(FIELDS):
        for v in range(tiles):
            last[f, pl.ds(v * TILE, TILE)] = state[f * tiles + v]

    def store(c):
        here = pl.ds(c * STEP, STEP)
        return pltpu.make_async_copy(sweep.at[here], base.at[here], sems.at[0, c])

    def backward(t, carry):
        state = list(carry)
        for i in range(STEP):
            j = rows - 1 - (t * STEP + i)
            for f in range(FIELDS):
                p, m = piv[f, j], bwd[f, j]
                for v in range(tiles):
                    k = f * tiles + v
                    here = pl.ds(v * TILE, TILE)
                    state[k] = p * sweep[j, f, here] + m * state[k]
                    sweep[j, f, here] = state[k]
        store(chunks - 1 - t).start()
        return tuple(state)

    state = lax.fori_loop(0, chunks, backward, start)
    for f in range(FIELDS):
        for v in range(tiles):
            first[f, pl.ds(v * TILE, TILE)] = state[f * tiles + v]
    walls[0] = weight[0]
    walls[1] = weight[rows - 1]
    for c in range(chunks):
        store(c).wait()


def edges(side, last, first, rim, walls, inner, outer, near, far, fwd, piv, bwd, fix, packed, entry, resp, ends):
    nf, span, lanes = last.shape
    rows = fix.shape[0]
    tiles = span // TILE
    tile = (TILE, lanes)
    sub = row_of(tile)
    low, high = sub == 0, sub == TILE - 1
    upper = sub < FIELDS
    flip = jnp.broadcast_to(side[0], tile) == 1
    even = jnp.broadcast_to(side[1], tile) == 0
    zero, one = jnp.zeros(tile, f32), jnp.ones(tile, f32)
    twice = lambda x: jnp.concatenate([x, x], axis=0)
    fwd8, piv8, bwd8 = twice(fwd[...]), twice(piv[...]), twice(bwd[...])
    column = lambda x, j: jnp.broadcast_to(x[:, j : j + 1], tile)

    state, q = zero, one
    prods = []
    for j in range(rows):
        x = jnp.where(upper == flip, twice(inner[j, :, 0]), twice(outer[j, :, 0]))
        m = column(fwd8, j)
        state = rim[j] * x + m * state
        fix[j] = state
        if j:
            q = q * m
        resp[j] = q
    top, a, r = zero, zero, one
    for j in reversed(range(rows)):
        p, m = column(piv8, j), column(bwd8, j)
        top = p * fix[j] + m * top
        fix[j] = top
        a = p * resp[j] + m * a
        if j < rows - 1:
            r = r * m
        resp[j] = jnp.where(upper, a, r)
    enters, leaves, lift = column(fwd8, 0), column(bwd8, rows - 1), column(piv8, rows - 1)
    ends[...] = jnp.where(upper, enters, leaves)

    for f in range(FIELDS):
        one_row = lambda x: x[f : f + 1]
        for v in range(tiles):
            here = pl.ds(v * TILE, TILE)
            below = jnp.where(even, far[f, here], near[f, here])
            above = jnp.where(even, near[f, here], far[f, here])
            under = walls[0, here] * below
            over = walls[1, here] * above
            lifted = one_row(lift) * over
            value = last[f, here] + one_row(q) * under + over
            answer = first[f, here] + one_row(a) * under + one_row(r) * lifted
            if v == 0:
                value = value + jnp.where(low, state[f : f + 1], 0.0)
                answer = answer + jnp.where(low, top[f : f + 1], 0.0)
            if v == tiles - 1:
                value = value + jnp.where(high, state[FIELDS + f : FIELDS + f + 1], 0.0)
                answer = answer + jnp.where(high, top[FIELDS + f : FIELDS + f + 1], 0.0)
            entry[0, f, here] = under
            entry[1, f, here] = lifted
            packed[pl.ds(v * TILE * ROWS + f, TILE, stride=ROWS)] = value
            packed[pl.ds(v * TILE * ROWS + FIELDS + f, TILE, stride=ROWS)] = answer
    group = lane_of(tile) // COEF_LANES
    out = zero
    for i, c in enumerate((q * enters, a * enters, r * leaves)):
        for f in range(FIELDS):
            out = jnp.where(group == i * FIELDS + f, c[f : f + 1], out)
    for v in range(tiles):
        packed[pl.ds(v * TILE * ROWS + 2 * FIELDS, TILE, stride=ROWS)] = out


def solve(got, out):
    count = got.shape[0] // ROWS
    tile = (TILE, got.shape[1])
    sub, lane = row_of(tile), lane_of(tile)
    upper = sub < FIELDS
    zero = jnp.zeros(tile, f32)

    def coefficient(k, i):
        here = lane == (i * FIELDS + sub % FIELDS) * COEF_LANES
        row = jnp.broadcast_to(got[pl.ds(k * ROWS + 2 * FIELDS, 1)], tile)
        return jnp.broadcast_to(jnp.sum(jnp.where(here, row, 0.0), axis=1, keepdims=True), tile)

    e, entering = zero, []
    for k in range(count):
        both = got[pl.ds(k * ROWS, TILE)]
        entering.append(e)
        out[k] = e
        e = jnp.where(upper, both, pltpu.roll(both, FIELDS, 0)) + coefficient(k, 0) * e
    b = zero
    for k in reversed(range(count)):
        both = got[pl.ds(k * ROWS, TILE)]
        e = out[k]
        out[k] = jnp.where(upper, e, b)
        b = jnp.where(upper, pltpu.roll(both, FIELDS, 0), both) + coefficient(k, 1) * e + coefficient(k, 2) * b


def finish(base, got, entry, resp, fix, ends, out, start, stage, sems):
    rows, _, span, lanes = out.shape
    tiles = span // TILE
    sub = row_of((TILE, lanes))
    chunks = rows // STEP

    def load(c):
        here = pl.ds(c * STEP, STEP)
        return pltpu.make_async_copy(base.at[here], stage.at[here], sems.at[0, c])

    def store(c):
        here = pl.ds(c * STEP, STEP)
        return pltpu.make_async_copy(stage.at[here], out.at[here], sems.at[1, c])

    for c in range(chunks):
        load(c).start()
    for f in range(FIELDS):
        for v in range(tiles):
            here = pl.ds(v * TILE, TILE)
            e = got[pl.ds(v * TILE * TILE + f, TILE, stride=TILE)]
            b = got[pl.ds(v * TILE * TILE + FIELDS + f, TILE, stride=TILE)]
            start[0, f, here] = ends[pl.ds(f, 1)] * e + entry[0, f, here]
            start[1, f, here] = ends[pl.ds(FIELDS + f, 1)] * b + entry[1, f, here]

    def body(c, carry):
        load(c).wait()
        for f in range(FIELDS):
            u = [start[0, f, pl.ds(v * TILE, TILE)] for v in range(tiles)]
            w = [start[1, f, pl.ds(v * TILE, TILE)] for v in range(tiles)]
            for i in range(STEP):
                j = c * STEP + i
                a, r = resp[j, pl.ds(f, 1)], resp[j, pl.ds(FIELDS + f, 1)]
                for v in range(tiles):
                    here = pl.ds(v * TILE, TILE)
                    x = stage[j, f, here] + a * u[v] + r * w[v]
                    if v == 0:
                        x = x + jnp.where(sub == 0, fix[j, pl.ds(f, 1)], 0.0)
                    if v == tiles - 1:
                        x = x + jnp.where(sub == TILE - 1, fix[j, pl.ds(FIELDS + f, 1)], 0.0)
                    stage[j, f, here] = x
        store(c).start()
        return carry

    lax.fori_loop(0, chunks, body, 0)
    for c in range(chunks):
        store(c).wait()


def params(mib):
    return pltpu.CompilerParams(vmem_limit_bytes=mib << 20)


def on_device(fields, kappa, fwd, piv, bwd):
    rows, nf, span, lanes = fields.shape
    shape = lambda *s: jax.ShapeDtypeStruct(s, f32)
    in_hbm = lambda x: pltpu.with_memory_space_constraint(x, pltpu.HBM)
    count = lax.axis_size(GY)
    around = lax.axis_size(GZ)
    pairs = lambda n, first: [(i, i + 1) for i in range(first, n - 1, 2)]
    both = lambda ends: ends + [(b, a) for a, b in ends]
    side = jnp.stack([lax.axis_index("c"), lax.rem(lax.axis_index("z"), 2)]).astype(jnp.int32)
    fwd, piv, bwd = fwd.T, piv.T, bwd.T
    fields, kappa = in_hbm(fields), in_hbm(kappa)
    inner, outer, near, far = pl.pallas_call(
        collect,
        out_shape=(shape(rows, nf, 1, lanes),) * 2 + (shape(nf, span, lanes),) * 2,
        in_specs=[SMEM, HBM],
        out_specs=(VMEM,) * 4,
        scratch_shapes=[pltpu.SemaphoreType.DMA((4,))],
        compiler_params=params(4),
        name="collect",
    )(side, fields)
    outer = lax.ppermute(outer, GZ, both(pairs(around, 1) + [(around - 1, 0)]))
    far = lax.ppermute(far, GY, both(pairs(count, 1)))
    near = lax.ppermute(near, GY, both(pairs(count, 0)))
    inner = lax.ppermute(inner, GZ, both(pairs(around, 0)))

    chunks = rows // STEP
    base, last, first, rim, walls = pl.pallas_call(
        interior,
        out_shape=(
            pltpu.HBM((rows, nf, span, lanes), f32),
            shape(nf, span, lanes),
            shape(nf, span, lanes),
            shape(rows, TILE, lanes),
            shape(2, span, lanes),
        ),
        in_specs=[HBM, HBM, SMEM, SMEM, SMEM],
        out_specs=(HBM,) + (VMEM,) * 4,
        scratch_shapes=[
            pltpu.VMEM((rows + 2, nf, span, lanes), f32),
            pltpu.VMEM((rows, span, lanes), f32),
            pltpu.VMEM((rows, nf, span, lanes), f32),
            pltpu.SemaphoreType.DMA((2, chunks)),
        ],
        compiler_params=params(24),
        cost_estimate=pl.CostEstimate(flops=20 * fields.size, bytes_accessed=9 * fields.size, transcendentals=0),
        name="interior",
    )(fields, kappa, fwd, piv, bwd)

    fix, packed, entry, resp, ends = pl.pallas_call(
        edges,
        out_shape=(
            shape(rows, TILE, lanes),
            shape(span * ROWS, lanes),
            shape(2, nf, span, lanes),
            shape(rows, TILE, lanes),
            shape(TILE, lanes),
        ),
        in_specs=[SMEM] + [VMEM] * 11,
        out_specs=(VMEM,) * 5,
        compiler_params=params(4),
        name="edges",
    )(side, last, first, rim, walls, inner, outer, near, far, fwd, piv, bwd)

    got = lax.all_to_all(packed.reshape(count, ROWS, 1, lanes), GY, 0, 0)
    out = pl.pallas_call(
        solve,
        out_shape=shape(count, TILE, lanes),
        in_specs=[VMEM],
        out_specs=VMEM,
        compiler_params=params(4),
        name="solve",
    )(got.reshape(count * ROWS, lanes))
    back = lax.all_to_all(out, GY, 0, 0)
    return pl.pallas_call(
        finish,
        out_shape=shape(rows, nf, span, lanes),
        in_specs=[HBM] + [VMEM] * 5,
        out_specs=HBM,
        scratch_shapes=[
            pltpu.VMEM((2, nf, span, lanes), f32),
            pltpu.VMEM((rows, nf, span, lanes), f32),
            pltpu.SemaphoreType.DMA((2, chunks)),
        ],
        compiler_params=params(16),
        name="finish",
    )(in_hbm(base), back.reshape(count * TILE, lanes), entry, resp, fix, ends)


def solution(mesh):
    nz = 8 if mesh.shape["gy"] % 8 == 0 else 1
    split = Mesh(mesh.devices.reshape(-1, nz, mesh.shape["gz"] // 2, 2), GY + GZ)
    placed = (P(GY, None, GZ, None), P(GY, GZ, None), P(GY, None), P(GY, None), P(GY, None))
    return jax.shard_map(
        on_device, mesh=split, in_specs=placed, out_specs=P(GY, None, GZ, None), check_vma=False
    )
```

time: 292 us -> 54.9 us (0.19)
  waiting for transfers between devices: 77.9 us -> 0.01 us
  blocking collectives: 106 us -> 37.4 us
  other arithmetic: 48.8 us -> 0.08 us
  local copies, waits for them, and re-layouts: 26.5 us -> 0.01 us
  between operations: 13.6 us -> 0.11 us
  Pallas kernels: 0 us -> 13.2 us
  matrix products: 10.4 us -> 0 us
  starting transfers between devices: 6.58 us -> 3.3 us
    all_gather x2 -> x0, blocking collectives: 106 us -> none  [entering_2(): gathered = jax.tree.map(lambda a: lax.all_gather(a, axis), part)]
    all_gather x2 -> x0, waiting for transfers between devices: 77.9 us -> none  [entering_2(): gathered = jax.tree.map(lambda a: lax.all_gather(a, axis), part)]
    add x34 -> x0, other arithmetic: 48.4 us -> none  [the longest x31 28.6 us: combine(): return (earlier[0] * later[0], earlier[1] * later[0] + later[1])]
    all_to_all x0 -> x2, blocking collectives: none -> 37.4 us  [the longest x1 23.5 us: on_device(): got = lax.all_to_all(packed.reshape(count, ROWS, 1, lanes), GY, 0, 0)]
    pallas_call x0 -> x5, Pallas kernels: none -> 13.2 us  [the longest x1 6.93 us: on_device(): pl.pallas_call(interior, out_shape=(pltpu.HBM((rows, nf, span, lanes), f3...]
    slice x7 -> x0, local copies, waits for them, and re-layouts: 11.9 us -> none  [the longest x2 9.21 us: on_device(): stream_sum = jnp.roll(fields, 1, 3) + jnp.roll(fields, -1, 3)]
    dot_general x2 -> x0, matrix products: 10.4 us -> none  [local_rows(): jnp.einsum('ijf,jfzx->ifzx', weights, values, precision=lax.Precision.HIG...]
    unnamed x19 -> x6, local copies, waits for them, and re-layouts: 9.37 us -> 0.01 us
  transfers between devices with their start and end apart: 6 -> 4, of which waited for: 2 -> 0; matrix products, arithmetic and copies ran while one was open for 4% -> 0% of each run, Pallas kernels for 0% -> 13%
where the time goes in v1:
time: 54.9 us; the launch traced here: 54.1 us
  blocking collectives  37.4 us (68%)
  Pallas kernels  13.2 us (24%)
  starting transfers between devices  3.3 us (6%)
    all_to_all x1, blocking collectives, on_device(): got = lax.all_to_all(packed.reshape(count, ROWS, 1, lanes), GY, 0, 0)  23.5 us
    all_to_all x1, blocking collectives, on_device(): back = lax.all_to_all(out, GY, 0, 0)  13.9 us
    pallas_call x1, Pallas kernels, on_device(): pl.pallas_call(interior, out_shape=(pltpu.HBM((rows, nf, span, lanes), f3...  6.93 us
    pallas_call x1, Pallas kernels, on_device(): pl.pallas_call(finish, out_shape=shape(rows, nf, span, lanes), in_specs=[...  3.45 us
    ppermute x1, starting transfers between devices, on_device(): outer = lax.ppermute(outer, GZ, both(pairs(around, 1) + [(around - 1, 0)]))  2.36 us
    pallas_call x1, Pallas kernels, on_device(): pl.pallas_call(collect, out_shape=(shape(rows, nf, 1, lanes),) * 2 + (sha...  1.61 us
  transfers between devices with their start and end apart: 4, of which 0 were waited for; matrix products, arithmetic and copies ran while one was open for 0% of the time, Pallas kernels for 13%

profile of v1, /device:TPU:2, one launch (start us, length us, event | category | flops | bytes accessed | tf_op | source)
XLA Modules:
  0.0 54.1 jit_solution(5150093208507225296)
XLA Ops:
  0.0 0.0 copy-start.2
  0.0 0.0 copy-start.1
  0.0 0.0 copy-start
  0.0 0.1 pad_add_fusion.side
  0.1 1.6 %collect.1 = (f32[64,4,1,128]{3,2,1,0:T(1,128)S(1)}, f32[64,4,1,128]{3,2,1,0:T(1,128)S(1)}, f32[4,32,128]{2,1,0:T(8,128)S(1)}, f32[4,32,128]{2,1,0:T(8,128)S(1)}) custom-call(s32[2]{0:T(128)S(1)} %pad_add_fusion.side, f32[64,4,32,128]{3,2,1,0:T(8,128)} %fields.3), custom_call_target="tpu_custom_call" | custom-call | tf_op jit(solution)/shard_map/collect/pallas_call | solution.py:299
  1.7 0.1 collective-permute-start
  1.8 2.4 %collective-permute-start.1 = (f32[64,4,1,128]{3,2,1,0:T(1,128)S(1)}, f32[64,4,1,128]{3,2,1,0:T(1,128)S(1)}, u32[]{:S(2)}, u32[]{:S(2)}) collective-permute-start(f32[64,4,1,128]{3,2,1,0:T(1,128)S(1)} %get-tuple-element.25), channel_id=1, source_target_pairs={{1,2},{3,4},{5,6},{7,0},{2,1},{4,3},{6,5},{0,7},{9,10},{11,12},{13... | collective-permute-start | bytes 393224 | tf_op jit(solution)/shard_map/ppermute | solution.py:308
  4.2 0.2 collective-permute-start.2
  4.4 0.7 %collective-permute-start.3 = (f32[4,32,128]{2,1,0:T(8,128)S(1)}, f32[4,32,128]{2,1,0:T(8,128)S(1)}, u32[]{:S(2)}, u32[]{:S(2)}) collective-permute-start(f32[4,32,128]{2,1,0:T(8,128)S(1)} %get-tuple-element.27), channel_id=1, source_target_pairs={{8,16},{24,32},{40,48},{56,64},{72,80},{88,96},{104,112},{120,128}... | collective-permute-start | bytes 196616 | tf_op jit(solution)/shard_map/ppermute | solution.py:309
  5.0 0.0 copy-done.2
  5.0 0.0 copy-done.1
  5.0 0.0 copy-done
  5.1 6.9 %interior.1 = (f32[64,4,32,128]{3,2,1,0:T(8,128)}, f32[4,32,128]{2,1,0:T(8,128)S(1)}, f32[4,32,128]{2,1,0:T(8,128)S(1)}, f32[64,8,128]{2,1,0:T(8,128)S(1)}, f32[2,32,128]{2,1,0:T(8,128)S(1)}) custom-call(f32[64,4,32,128]{3,2,1,0:T(8,128)} %fields.3, f32[64,32,128]{2,1,0:T(8,128)} %kappa.1, f32[4,64]{1,0:T(4,128)S(1)} %bitcast.11, f32[4,64]{1,0:T(4,128)S(1)} %bitcast.13, ...), custom_call_target="tpu_custom_call" | custom-call | flops 20971520 | bytes 9437184 | tf_op jit(solution)/shard_map/interior/pallas_call | solution.py:314
  12.0 0.0 collective-permute-done.2.near
  12.0 0.0 collective-permute-done.3.far
  12.0 0.0 collective-permute-done.inner
  12.0 0.0 collective-permute-done.1.outer
  12.0 1.0 %edges.1 = (f32[64,8,128]{2,1,0:T(8,128)S(1)}, f32[288,128]{1,0:T(8,128)S(1)}, f32[2,4,32,128]{3,2,1,0:T(8,128)S(1)}, f32[64,8,128]{2,1,0:T(8,128)S(1)}, f32[8,128]{1,0:T(8,128)S(1)}) custom-call(s32[2]{0:T(128)S(1)} %pad_add_fusion.side, f32[4,32,128]{2,1,0:T(8,128)S(1)} %get-tuple-element.20.last, f32[4,32,128]{2,1,0:T(8,128)S(1)} %get-tuple-element.21.first, ...), custom_call_target="tpu_custom_call" | custom-call | tf_op jit(solution)/shard_map/edges/pallas_call | solution.py:336
  13.0 23.5 %all_to_all.10 = f32[32,9,1,128]{3,2,1,0:T(1,128)S(1)} all-to-all(f32[32,9,1,128]{3,2,1,0:T(1,128)S(1)} %bitcast.10), channel_id=1, replica_groups=mesh['y'=4,'z'=8,'x'=4,'c'=2] {'y','z'}, dimensions={0} | all-to-all | bytes 294912 | tf_op jit(solution)/shard_map/all_to_all | solution.py:351
  36.5 0.2 solve.1
  36.7 13.9 %all_to_all.11 = f32[32,8,128]{2,1,0:T(8,128)S(1)} all-to-all(f32[32,8,128]{2,1,0:T(8,128)S(1)} %solve.1), channel_id=1, replica_groups=mesh['y'=4,'z'=8,'x'=4,'c'=2] {'y','z'}, dimensions={0} | all-to-all | bytes 262144 | tf_op jit(solution)/shard_map/all_to_all | solution.py:360
  50.7 3.5 %finish.1 = f32[64,4,32,128]{3,2,1,0:T(8,128)} custom-call(f32[64,4,32,128]{3,2,1,0:T(8,128)} %get-tuple-element.19.base, f32[256,128]{1,0:T(8,128)S(1)} %bitcast.9, f32[2,4,32,128]{3,2,1,0:T(8,128)S(1)} %get-tuple-element.29.entry, f32[64,8,128]{2,1,0:T(8,128)S(1)} %get-tuple-element.30.resp, f32[64,8,128]{2,1,0:T(8,128)S(1)} %get-tuple-element.31.fix, ...), custom_call_target="tpu_custom_call" | custom-call | tf_op jit(solution)/shard_map/finish/pallas_call | solution.py:361
Async XLA Ops:
  0.0 5.0 %copy-start.2 = (f32[64,4]{0,1:T(4,128)S(1)}, f32[64,4]{0,1:T(4,128)}, u32[]{:S(2)}) copy-start(f32[64,4]{0,1:T(4,128)} %param.9) | copy-start | bytes 3076
  0.0 5.0 %copy-start.1 = (f32[64,4]{0,1:T(4,128)S(1)}, f32[64,4]{0,1:T(4,128)}, u32[]{:S(2)}) copy-start(f32[64,4]{0,1:T(4,128)} %param.8) | copy-start | bytes 3076
  0.0 5.0 %copy-start = (f32[64,4]{0,1:T(4,128)S(1)}, f32[64,4]{0,1:T(4,128)}, u32[]{:S(2)}) copy-start(f32[64,4]{0,1:T(4,128)} %param.7) | copy-start | bytes 3076
  1.7 10.3 %collective-permute-start = (f32[64,4,1,128]{3,2,1,0:T(1,128)S(1)}, f32[64,4,1,128]{3,2,1,0:T(1,128)S(1)}, u32[]{:S(2)}, u32[]{:S(2)}) collective-permute-start(f32[64,4,1,128]{3,2,1,0:T(1,128)S(1)} %get-tuple-element.24), channel_id=1, source_target_pairs={{0,1},{2,3},{4,5},{6,7},{1,0},{3,2},{5,4},{7,6},{8,9},{10,11},{12,... | collective-permute-start | bytes 393224 | tf_op jit(solution)/shard_map/ppermute | solution.py:311
  1.8 10.2 %collective-permute-start.1 = (f32[64,4,1,128]{3,2,1,0:T(1,128)S(1)}, f32[64,4,1,128]{3,2,1,0:T(1,128)S(1)}, u32[]{:S(2)}, u32[]{:S(2)}) collective-permute-start(f32[64,4,1,128]{3,2,1,0:T(1,128)S(1)} %get-tuple-element.25), channel_id=1, source_target_pairs={{1,2},{3,4},{5,6},{7,0},{2,1},{4,3},{6,5},{0,7},{9,10},{11,12},{13... | collective-permute-start | bytes 393224 | tf_op jit(solution)/shard_map/ppermute | solution.py:308
  4.2 7.8 %collective-permute-start.2 = (f32[4,32,128]{2,1,0:T(8,128)S(1)}, f32[4,32,128]{2,1,0:T(8,128)S(1)}, u32[]{:S(2)}, u32[]{:S(2)}) collective-permute-start(f32[4,32,128]{2,1,0:T(8,128)S(1)} %get-tuple-element.26), channel_id=1, source_target_pairs={{0,8},{16,24},{32,40},{48,56},{64,72},{80,88},{96,104},{112,120},{... | collective-permute-start | bytes 196616 | tf_op jit(solution)/shard_map/ppermute | solution.py:310
  4.4 7.6 %collective-permute-start.3 = (f32[4,32,128]{2,1,0:T(8,128)S(1)}, f32[4,32,128]{2,1,0:T(8,128)S(1)}, u32[]{:S(2)}, u32[]{:S(2)}) collective-permute-start(f32[4,32,128]{2,1,0:T(8,128)S(1)} %get-tuple-element.27), channel_id=1, source_target_pairs={{8,16},{24,32},{40,48},{56,64},{72,80},{88,96},{104,112},{120,128}... | collective-permute-start | bytes 196616 | tf_op jit(solution)/shard_map/ppermute | solution.py:309

commit v2 on v1

v2 whole, which is shorter than its diff:
```python
import jax
import jax.numpy as jnp
from jax import lax
from jax.experimental import pallas as pl
from jax.experimental.pallas import tpu as pltpu
from jax.sharding import Mesh
from jax.sharding import PartitionSpec as P

GY = ("y", "z")
GZ = ("x", "c")
FIELDS = 4
TILE = 8
STEP = 8
ROWS = 4 * FIELDS + 3

VMEM = pl.BlockSpec(memory_space=pltpu.VMEM)
SMEM = pl.BlockSpec(memory_space=pltpu.SMEM)
HBM = pl.BlockSpec(memory_space=pltpu.HBM)
f32 = jnp.float32


def row_of(shape):
    return lax.broadcasted_iota(jnp.int32, shape, 0)


def lane_of(shape):
    return lax.broadcasted_iota(jnp.int32, shape, 1)


def collect(side, fields, kappa, fwd, piv, bwd, weight, wide, inner, outer, sems):
    rows, _, span, lanes = fields.shape
    z_near = jnp.where(side[0] == 0, span - 1, 0)
    copies = [
        pltpu.make_async_copy(fields.at[:, :, pl.ds(span - 1 - z_near, 1)], outer, sems.at[0]),
        pltpu.make_async_copy(fields.at[:, :, pl.ds(z_near, 1)], inner, sems.at[1]),
        pltpu.make_async_copy(kappa, weight, sems.at[2]),
    ]
    for copy in copies:
        copy.start()
    for i, ref in enumerate((fwd, piv, bwd)):
        x = ref[...]
        x = jnp.concatenate([x, x], axis=0)
        for j in range(rows):
            wide[i, j] = jnp.broadcast_to(x[:, j : j + 1], (TILE, lanes))
    for copy in copies:
        copy.wait()


def forward(fields, weight, wide, sweep, state, layers, fresh):
    rows, _, span, lanes = sweep.shape
    tiles = span // TILE
    tile = (TILE, lanes)
    at = lambda v: pl.ds(v * TILE, TILE)
    sub = row_of(tile)
    total = rows // STEP
    layers[0] = fields[rows - 1]
    layers[1] = fields[0]

    def beside(j, f, v, x):
        if v == 0:
            low = jnp.where(sub == 0, 0.0, pltpu.roll(x, 1, 0))
        else:
            low = fields[j, f, pl.ds(v * TILE - 1, TILE)]
        if v == tiles - 1:
            return low + jnp.where(sub == TILE - 1, 0.0, pltpu.roll(x, TILE - 1, 0))
        return low + fields[j, f, pl.ds(v * TILE + 1, TILE)]

    def update(c):
        above_first = jnp.where(jnp.broadcast_to(c, tile) > 0, 1.0, 0.0)
        below_last = jnp.where(jnp.broadcast_to(c, tile) < total - 1, 1.0, 0.0)
        for v in range(tiles):
            under = [fields[jnp.maximum(c * STEP - 1, 0), f, at(v)] * above_first for f in range(FIELDS)]
            here = [fields[c * STEP, f, at(v)] for f in range(FIELDS)]
            for i in range(STEP):
                j = c * STEP + i
                k = weight[j, at(v)]
                own = 1.0 - 6.0 * k
                half = 0.5 * here[0]
                for f in range(FIELDS):
                    x = here[f]
                    if i < STEP - 1:
                        over = fields[j + 1, f, at(v)]
                    else:
                        over = fields[jnp.minimum(j + 1, rows - 1), f, at(v)] * below_last
                    around = beside(j, f, v, x)
                    around = around + (pltpu.roll(x, 1, 1) + pltpu.roll(x, lanes - 1, 1))
                    around = around + (under[f] + over)
                    new = own * x + k * around
                    if f == 2:
                        new = new + half
                    fresh[i, f, at(v)] = new
                    under[f], here[f] = x, over

    def advance(c, carry):
        carry = list(carry)
        for i in range(STEP):
            j = c * STEP + i
            for f in range(FIELDS):
                m = wide[0, j, pl.ds(f, 1)]
                for v in range(tiles):
                    k = f * tiles + v
                    carry[k] = fresh[i, f, at(v)] + m * carry[k]
                    sweep[j, f, at(v)] = carry[k]
        return tuple(carry)

    def both(c, carry):
        carry = advance(c - 1, carry)
        update(c)
        return carry

    update(0)
    carry = lax.fori_loop(1, total, both, (jnp.zeros(tile, f32),) * (FIELDS * tiles))
    carry = advance(total - 1, carry)
    for f in range(FIELDS):
        for v in range(tiles):
            state[f, at(v)] = carry[f * tiles + v]


def backward(wide, sweep, base, first):
    rows, _, span, lanes = base.shape
    tiles = span // TILE
    at = lambda v: pl.ds(v * TILE, TILE)

    def body(t, state):
        state = list(state)
        for i in range(2 * STEP):
            j = rows - 1 - (t * 2 * STEP + i)
            for f in range(FIELDS):
                p, m = wide[1, j, pl.ds(f, 1)], wide[2, j, pl.ds(f, 1)]
                for v in range(tiles):
                    k = f * tiles + v
                    state[k] = p * base[j, f, at(v)] + m * state[k]
                    base[j, f, at(v)] = state[k]
        return tuple(state)

    start = (jnp.zeros((TILE, lanes), f32),) * (FIELDS * tiles)
    state = lax.fori_loop(0, rows // (2 * STEP), body, start)
    for f in range(FIELDS):
        for v in range(tiles):
            first[f, at(v)] = state[f * tiles + v]


def edges(side, base_in, last, first, kappa, inner, outer, layers, wide, base, fix, packed, resp):
    del base_in, base
    nf, span, lanes = last.shape
    rows = fix.shape[0]
    tiles = span // TILE
    tile = (TILE, lanes)
    sub, lane = row_of(tile), lane_of(tile)
    low, high = sub == 0, sub == TILE - 1
    upper = sub < FIELDS
    flip = jnp.broadcast_to(side[0], tile) == 1
    zero, one = jnp.zeros(tile, f32), jnp.ones(tile, f32)
    twice = lambda x: jnp.concatenate([x, x], axis=0)

    state, q = zero, one
    for j in range(rows):
        x = jnp.where(upper == flip, twice(inner[j, :, 0]), twice(outer[j, :, 0]))
        k = jnp.where(upper, kappa[j, pl.ds(0, 1)], kappa[j, pl.ds(span - 1, 1)])
        m = wide[0, j]
        state = k * x + m * state
        fix[j] = state
        if j:
            q = q * m
        resp[j] = q
    top, a, r = zero, zero, one
    for j in reversed(range(rows)):
        p, m = wide[1, j], wide[2, j]
        top = p * fix[j] + m * top
        fix[j] = top
        a = p * resp[j] + m * a
        if j < rows - 1:
            r = r * m
        resp[j] = jnp.where(upper, a, r)

    for v in range(tiles):
        here = pl.ds(v * TILE, TILE)
        put = lambda i, x: packed.__setitem__(pl.ds(v * TILE * ROWS + i, TILE, stride=ROWS), x)
        for f in range(FIELDS):
            value, answer = last[f, here], first[f, here]
            if v == 0:
                value = value + jnp.where(low, state[f : f + 1], 0.0)
                answer = answer + jnp.where(low, top[f : f + 1], 0.0)
            if v == tiles - 1:
                value = value + jnp.where(high, state[FIELDS + f : FIELDS + f + 1], 0.0)
                answer = answer + jnp.where(high, top[FIELDS + f : FIELDS + f + 1], 0.0)
            put(f, value)
            put(FIELDS + f, answer)
            put(2 * FIELDS + f, layers[0, f, here])
            put(3 * FIELDS + f, layers[1, f, here])
        put(4 * FIELDS, kappa[0, here])
        put(4 * FIELDS + 1, kappa[rows - 1, here])
    enters, leaves, lift = wide[0, 0], wide[2, rows - 1], wide[1, rows - 1]
    coefs = (
        jnp.where(upper, q, r * lift),
        jnp.where(upper, one, a),
        q * enters,
        a * enters,
        r * leaves,
        jnp.where(upper, enters, leaves),
        jnp.where(upper, one, lift),
    )
    out = zero
    for i, c in enumerate(coefs):
        out = jnp.where(lane == i * TILE + sub, c, out)
    out = jnp.broadcast_to(jnp.sum(out, axis=0, keepdims=True), tile)
    for v in range(tiles):
        packed[pl.ds(v * TILE * ROWS + ROWS - 1, TILE, stride=ROWS)] = out


def solve(got, base_in, out, base, entry):
    del base_in, base
    count = got.shape[0] // ROWS
    tile = (TILE, got.shape[1])
    sub, lane = row_of(tile), lane_of(tile)
    upper = sub < FIELDS
    zero = jnp.zeros(tile, f32)
    swap = lambda x: pltpu.roll(x, FIELDS, 0)

    def coefficient(k, i):
        row = jnp.broadcast_to(got[pl.ds(k * ROWS + ROWS - 1, 1)], tile)
        row = jnp.where(lane == i * TILE + sub, row, 0.0)
        return jnp.broadcast_to(jnp.sum(row, axis=1, keepdims=True), tile)

    def layer(k):
        return got[pl.ds(k * ROWS + 2 * FIELDS, TILE)] if 0 <= k < count else zero

    e = zero
    for k in range(count):
        weight = jnp.where(upper, got[pl.ds(k * ROWS + 4 * FIELDS, 1)], got[pl.ds(k * ROWS + 4 * FIELDS + 1, 1)])
        brought = weight * jnp.where(upper, layer(k - 1), layer(k + 1))
        both = got[pl.ds(k * ROWS, TILE)] + coefficient(k, 0) * brought + coefficient(k, 1) * swap(brought)
        entry[0, k] = both
        entry[1, k] = coefficient(k, 6) * brought
        out[k] = e
        e = jnp.where(upper, both, swap(both)) + coefficient(k, 2) * e
    b = zero
    for k in reversed(range(count)):
        both, e = entry[0, k], out[k]
        out[k] = coefficient(k, 5) * jnp.where(upper, e, b) + entry[1, k]
        b = jnp.where(upper, swap(both), both) + coefficient(k, 3) * e + coefficient(k, 4) * b


def finish(base, got, resp, fix, out, start, stage, sems):
    rows, _, span, lanes = out.shape
    tiles = span // TILE
    sub = row_of((TILE, lanes))
    chunks = rows // STEP

    def store(c):
        here = pl.ds(c * STEP, STEP)
        return pltpu.make_async_copy(stage.at[here], out.at[here], sems.at[1, c])

    for f in range(FIELDS):
        for v in range(tiles):
            here = pl.ds(v * TILE, TILE)
            start[0, f, here] = got[pl.ds(v * TILE * TILE + f, TILE, stride=TILE)]
            start[1, f, here] = got[pl.ds(v * TILE * TILE + FIELDS + f, TILE, stride=TILE)]

    def body(c, carry):
        for f in range(FIELDS):
            u = [start[0, f, pl.ds(v * TILE, TILE)] for v in range(tiles)]
            w = [start[1, f, pl.ds(v * TILE, TILE)] for v in range(tiles)]
            for i in range(STEP):
                j = c * STEP + i
                a, r = resp[j, pl.ds(f, 1)], resp[j, pl.ds(FIELDS + f, 1)]
                for v in range(tiles):
                    here = pl.ds(v * TILE, TILE)
                    x = base[j, f, here] + a * u[v] + r * w[v]
                    if v == 0:
                        x = x + jnp.where(sub == 0, fix[j, pl.ds(f, 1)], 0.0)
                    if v == tiles - 1:
                        x = x + jnp.where(sub == TILE - 1, fix[j, pl.ds(FIELDS + f, 1)], 0.0)
                    stage[j, f, here] = x
        store(c).start()
        return carry

    lax.fori_loop(0, chunks, body, 0)
    for c in range(chunks):
        store(c).wait()


def params(mib):
    return pltpu.CompilerParams(vmem_limit_bytes=mib << 20)


def on_device(fields, kappa, fwd, piv, bwd):
    rows, nf, span, lanes = fields.shape
    shape = lambda *s: jax.ShapeDtypeStruct(s, f32)
    vmem = lambda *s: pltpu.VMEM(s, f32)
    in_vmem = lambda x: pltpu.with_memory_space_constraint(x, pltpu.VMEM)
    in_hbm = lambda x: pltpu.with_memory_space_constraint(x, pltpu.HBM)
    count = lax.axis_size(GY)
    around = lax.axis_size(GZ)
    pairs = lambda n, first: [(i, i + 1) for i in range(first, n - 1, 2)]
    both = lambda ends: ends + [(b, a) for a, b in ends]
    side = lax.axis_index("c").astype(jnp.int32).reshape(1)
    fwd, piv, bwd = fwd.T, piv.T, bwd.T
    fields, kappa = in_hbm(fields), in_hbm(kappa)
    chunks = rows // STEP
    weight, wide, inner, outer = pl.pallas_call(
        collect,
        out_shape=(
            vmem(rows, span, lanes),
            vmem(3, rows, TILE, lanes),
            vmem(rows, nf, 1, lanes),
            vmem(rows, nf, 1, lanes),
        ),
        in_specs=[SMEM, HBM, HBM, VMEM, VMEM, VMEM],
        out_specs=(VMEM,) * 4,
        scratch_shapes=[pltpu.SemaphoreType.DMA((3,))],
        compiler_params=params(4),
        name="collect",
    )(side, *map(in_hbm, (fields, kappa, fwd, piv, bwd)))
    outer = lax.ppermute(outer, GZ, both(pairs(around, 1) + [(around - 1, 0)]))
    inner = lax.ppermute(inner, GZ, both(pairs(around, 0)))
    block = in_vmem(fields), in_vmem(weight), in_vmem(wide)
    sweep, last, layers = pl.pallas_call(
        forward,
        out_shape=(vmem(rows, nf, span, lanes), vmem(nf, span, lanes), vmem(2, nf, span, lanes)),
        in_specs=[VMEM] * 3,
        out_specs=(VMEM,) * 3,
        scratch_shapes=[pltpu.VMEM((STEP, nf, span, lanes), f32)],
        compiler_params=params(4),
        cost_estimate=pl.CostEstimate(flops=20 * fields.size, bytes_accessed=4 * fields.size, transcendentals=0),
        name="forward",
    )(*block)
    base, first = pl.pallas_call(
        backward,
        out_shape=(vmem(rows, nf, span, lanes), vmem(nf, span, lanes)),
        in_specs=[VMEM, VMEM],
        out_specs=(VMEM, VMEM),
        input_output_aliases={1: 0},
        compiler_params=params(4),
        cost_estimate=pl.CostEstimate(flops=1, bytes_accessed=1, transcendentals=0),
        name="backward",
    )(in_vmem(wide), in_vmem(sweep))

    base, fix, packed, resp = pl.pallas_call(
        edges,
        out_shape=(
            vmem(rows, nf, span, lanes),
            shape(rows, TILE, lanes),
            shape(span * ROWS, lanes),
            shape(rows, TILE, lanes),
        ),
        in_specs=[SMEM] + [VMEM] * 8,
        out_specs=(VMEM,) * 4,
        input_output_aliases={1: 0},
        compiler_params=params(4),
        name="edges",
    )(side, in_vmem(base), last, first, in_vmem(weight), inner, outer, layers, in_vmem(wide))

    got = lax.all_to_all(packed.reshape(count, ROWS, 1, lanes), GY, 0, 0)
    out, base = pl.pallas_call(
        solve,
        out_shape=(shape(count, TILE, lanes), pltpu.VMEM((rows, nf, span, lanes), f32)),
        in_specs=[VMEM, VMEM],
        out_specs=(VMEM, VMEM),
        input_output_aliases={1: 1},
        scratch_shapes=[pltpu.VMEM((2, count, TILE, lanes), f32)],
        compiler_params=params(4),
        name="solve",
    )(got.reshape(count * ROWS, lanes), in_vmem(base))
    back = lax.all_to_all(out, GY, 0, 0)
    return pl.pallas_call(
        finish,
        out_shape=shape(rows, nf, span, lanes),
        in_specs=[VMEM] * 4,
        out_specs=HBM,
        scratch_shapes=[
            pltpu.VMEM((2, nf, span, lanes), f32),
            pltpu.VMEM((rows, nf, span, lanes), f32),
            pltpu.SemaphoreType.DMA((2, chunks)),
        ],
        compiler_params=params(16),
        name="finish",
    )(in_vmem(base), back.reshape(count * TILE, lanes), resp, fix)


def solution(mesh):
    nz = 8 if mesh.shape["gy"] % 8 == 0 else 1
    split = Mesh(mesh.devices.reshape(-1, nz, mesh.shape["gz"] // 2, 2), GY + GZ)
    placed = (P(GY, None, GZ, None), P(GY, GZ, None), P(GY, None), P(GY, None), P(GY, None))
    return jax.shard_map(
        on_device, mesh=split, in_specs=placed, out_specs=P(GY, None, GZ, None), check_vma=False
    )
```

time: 54.9 us -> 50.8 us (0.925)
  Pallas kernels: 13.2 us -> 8.82 us
  blocking collectives: 37.4 us -> 38.8 us
  starting transfers between devices: 3.3 us -> 2.46 us
    pallas_call x4 -> x5, Pallas kernels: 9.75 us -> 6.56 us  [the longest x1 2.86 us: on_device(): pl.pallas_call(forward, out_shape=(vmem(rows, nf, span, lanes), vmem(nf,...]
    all_to_all x1, blocking collectives: 13.9 us -> 15.5 us  [on_device(): back = lax.all_to_all(out, GY, 0, 0)]
    pallas_call x1, Pallas kernels: 3.45 us -> 2.25 us  [on_device(): pl.pallas_call(finish, out_shape=shape(rows, nf, span, lanes), in_specs=[...]
    ppermute x2 -> x0, starting transfers between devices: 0.84 us -> none  [the longest x1 0.65 us: on_device(): far = lax.ppermute(far, GY, both(pairs(count, 1)))]
  transfers between devices with their start and end apart: 4 -> 2, of which waited for: 0 -> 0; matrix products, arithmetic and copies ran while one was open for 0% -> 0% of each run, Pallas kernels for 13% -> 7%
where the time goes in v2:
time: 50.8 us; the launch traced here: 50.1 us
  blocking collectives  38.8 us (76%)
  Pallas kernels  8.82 us (17%)
  starting transfers between devices  2.46 us (5%)
    all_to_all x1, blocking collectives, on_device(): got = lax.all_to_all(packed.reshape(count, ROWS, 1, lanes), GY, 0, 0)  23.2 us
    all_to_all x1, blocking collectives, on_device(): back = lax.all_to_all(out, GY, 0, 0)  15.5 us
    pallas_call x1, Pallas kernels, on_device(): pl.pallas_call(forward, out_shape=(vmem(rows, nf, span, lanes), vmem(nf,...  2.86 us
    pallas_call x1, Pallas kernels, on_device(): pl.pallas_call(collect, out_shape=(vmem(rows, span, lanes), vmem(3, rows,...  2.46 us
    ppermute x1, starting transfers between devices, on_device(): outer = lax.ppermute(outer, GZ, both(pairs(around, 1) + [(around - 1, 0)]))  2.37 us
    pallas_call x1, Pallas kernels, on_device(): pl.pallas_call(finish, out_shape=shape(rows, nf, span, lanes), in_specs=[...  2.25 us
  transfers between devices with their start and end apart: 2, of which 0 were waited for; matrix products, arithmetic and copies ran while one was open for 0% of the time, Pallas kernels for 7%

profile of v2, /device:TPU:2, one launch (start us, length us, event | category | flops | bytes accessed | tf_op | source)
XLA Modules:
  0.0 50.1 jit_solution(8100321128610631542)
XLA Ops:
  0.0 0.0 copy-start
  0.0 2.5 %collect.1 = (f32[64,32,128]{2,1,0:T(8,128)S(1)}, f32[3,64,8,128]{3,2,1,0:T(8,128)S(1)}, f32[64,4,1,128]{3,2,1,0:T(1,128)S(1)}, f32[64,4,1,128]{3,2,1,0:T(1,128)S(1)}) custom-call(s32[1]{0:T(128)} %bitcast.side, f32[64,4,32,128]{3,2,1,0:T(8,128)} %fields.3, f32[64,32,128]{2,1,0:T(8,128)} %kappa.1, f32[4,64]{1,0:T(4,128)} %bitcast.10, f32[4,64]{1,0:T(4,128)} %bitcast.11, ...), custom_call_target="tpu_custom_call" | custom-call | tf_op jit(solution)/shard_map/collect/pallas_call | solution.py:301
  2.5 0.1 collective-permute-start
  2.6 2.4 %collective-permute-start.1 = (f32[64,4,1,128]{3,2,1,0:T(1,128)S(1)}, f32[64,4,1,128]{3,2,1,0:T(1,128)S(1)}, u32[]{:S(2)}, u32[]{:S(2)}) collective-permute-start(f32[64,4,1,128]{3,2,1,0:T(1,128)S(1)} %get-tuple-element.27), channel_id=1, source_target_pairs={{1,2},{3,4},{5,6},{7,0},{2,1},{4,3},{6,5},{0,7},{9,10},{11,12},{13... | collective-permute-start | bytes 393224 | tf_op jit(solution)/shard_map/ppermute | solution.py:315
  4.9 0.0 copy-done
  4.9 2.9 %forward.1 = (f32[64,4,32,128]{3,2,1,0:T(8,128)S(1)}, f32[4,32,128]{2,1,0:T(8,128)S(1)}, f32[2,4,32,128]{3,2,1,0:T(8,128)S(1)}) custom-call(f32[64,4,32,128]{3,2,1,0:T(8,128)S(1)} %copy-done, f32[64,32,128]{2,1,0:T(8,128)S(1)} %get-tuple-element.21.weight.kappa, f32[3,64,8,128]{3,2,1,0:T(8,128)S(1)} %get-tuple-element.20.wide), custom_call_target="tpu_custom_call" | custom-call | flops 20971520 | bytes 4194304 | tf_op jit(solution)/shard_map/forward/pallas_call | solution.py:318
  7.8 0.6 %backward.1 = (f32[64,4,32,128]{3,2,1,0:T(8,128)S(1)}, f32[4,32,128]{2,1,0:T(8,128)S(1)}) custom-call(f32[3,64,8,128]{3,2,1,0:T(8,128)S(1)} %get-tuple-element.20.wide, f32[64,4,32,128]{3,2,1,0:T(8,128)S(1)} %get-tuple-element.22.sweep), custom_call_target="tpu_custom_call", output_to_operand_aliasing={{0}: (1, {})} | custom-call | flops 1 | bytes 1 | tf_op jit(solution)/shard_map/backward/pallas_call | solution.py:328
  8.4 0.0 collective-permute-done.inner
  8.4 0.0 collective-permute-done.1.outer
  8.4 0.4 edges.1
  8.8 23.2 %all_to_all.10 = f32[32,19,1,128]{3,2,1,0:T(1,128)S(1)} all-to-all(f32[32,19,1,128]{3,2,1,0:T(1,128)S(1)} %bitcast.9), channel_id=1, replica_groups=mesh['y'=4,'z'=8,'x'=4,'c'=2] {'y','z'}, dimensions={0} | all-to-all | bytes 622592 | tf_op jit(solution)/shard_map/all_to_all | solution.py:354
  32.0 0.3 solve.1
  32.3 15.5 %all_to_all.11 = f32[32,8,128]{2,1,0:T(8,128)S(1)} all-to-all(f32[32,8,128]{2,1,0:T(8,128)S(1)} %get-tuple-element.32), channel_id=1, replica_groups=mesh['y'=4,'z'=8,'x'=4,'c'=2] {'y','z'}, dimensions={0} | all-to-all | bytes 262144 | tf_op jit(solution)/shard_map/all_to_all | solution.py:365
  47.9 2.3 %finish.1 = f32[64,4,32,128]{3,2,1,0:T(8,128)} custom-call(f32[64,4,32,128]{3,2,1,0:T(8,128)S(1)} %get-tuple-element.31.base, f32[256,128]{1,0:T(8,128)S(1)} %bitcast.8, f32[64,8,128]{2,1,0:T(8,128)S(1)} %get-tuple-element.33.resp, f32[64,8,128]{2,1,0:T(8,128)S(1)} %get-tuple-element.34.fix), custom_call_target="tpu_custom_call" | custom-call | tf_op jit(solution)/shard_map/finish/pallas_call | solution.py:366
Async XLA Ops:
  0.0 4.9 %copy-start = (f32[64,4,32,128]{3,2,1,0:T(8,128)S(1)}, f32[64,4,32,128]{3,2,1,0:T(8,128)}, u32[]{:S(2)}) copy-start(f32[64,4,32,128]{3,2,1,0:T(8,128)} %fields.3) | copy-start | bytes 12582916
  2.5 5.9 %collective-permute-start = (f32[64,4,1,128]{3,2,1,0:T(1,128)S(1)}, f32[64,4,1,128]{3,2,1,0:T(1,128)S(1)}, u32[]{:S(2)}, u32[]{:S(2)}) collective-permute-start(f32[64,4,1,128]{3,2,1,0:T(1,128)S(1)} %get-tuple-element.26), channel_id=1, source_target_pairs={{0,1},{2,3},{4,5},{6,7},{1,0},{3,2},{5,4},{7,6},{8,9},{10,11},{12,... | collective-permute-start | bytes 393224 | tf_op jit(solution)/shard_map/ppermute | solution.py:316
  2.6 5.8 %collective-permute-start.1 = (f32[64,4,1,128]{3,2,1,0:T(1,128)S(1)}, f32[64,4,1,128]{3,2,1,0:T(1,128)S(1)}, u32[]{:S(2)}, u32[]{:S(2)}) collective-permute-start(f32[64,4,1,128]{3,2,1,0:T(1,128)S(1)} %get-tuple-element.27), channel_id=1, source_target_pairs={{1,2},{3,4},{5,6},{7,0},{2,1},{4,3},{6,5},{0,7},{9,10},{11,12},{13... | collective-permute-start | bytes 393224 | tf_op jit(solution)/shard_map/ppermute | solution.py:315

commit v3 on v2

--- a/solution.py
+++ b/solution.py
@@ -27,7 +27,7 @@
     return lax.broadcasted_iota(jnp.int32, shape, 1)
 
 
-def collect(side, fields, kappa, fwd, piv, bwd, weight, wide, inner, outer, sems):
+def collect(side, fields, kappa, fwd, piv, bwd, weight, wide, inner, outer, narrow, sems):
     rows, _, span, lanes = fields.shape
     z_near = jnp.where(side[0] == 0, span - 1, 0)
     copies = [
@@ -35,10 +35,13 @@
         pltpu.make_async_copy(fields.at[:, :, pl.ds(z_near, 1)], inner, sems.at[1]),
         pltpu.make_async_copy(kappa, weight, sems.at[2]),
     ]
-    for copy in copies:
+    small = [pltpu.make_async_copy(ref, narrow.at[i], sems.at[3 + i]) for i, ref in enumerate((fwd, piv, bwd))]
+    for copy in small + copies:
         copy.start()
-    for i, ref in enumerate((fwd, piv, bwd)):
-        x = ref[...]
+    for copy in small:
+        copy.wait()
+    for i in range(3):
+        x = narrow[i]
         x = jnp.concatenate([x, x], axis=0)
         for j in range(rows):
             wide[i, j] = jnp.broadcast_to(x[:, j : j + 1], (TILE, lanes))
@@ -306,9 +309,9 @@
             vmem(rows, nf, 1, lanes),
             vmem(rows, nf, 1, lanes),
         ),
-        in_specs=[SMEM, HBM, HBM, VMEM, VMEM, VMEM],
+        in_specs=[SMEM] + [HBM] * 5,
         out_specs=(VMEM,) * 4,
-        scratch_shapes=[pltpu.SemaphoreType.DMA((3,))],
+        scratch_shapes=[pltpu.VMEM((3, nf, rows), f32), pltpu.SemaphoreType.DMA((6,))],
         compiler_params=params(4),
         name="collect",
     )(side, *map(in_hbm, (fields, kappa, fwd, piv, bwd)))

time: 50.8 us -> 49.9 us (0.982)
  Pallas kernels: 8.82 us -> 7.99 us
    pallas_call x1, Pallas kernels: 2.46 us -> 1.63 us  [on_device(): pl.pallas_call(collect, out_shape=(vmem(rows, span, lanes), vmem(3, rows,...]
where the time goes in v3:
time: 49.9 us; the launch traced here: 49.3 us
  blocking collectives  38.8 us (78%)
  Pallas kernels  7.99 us (16%)
  starting transfers between devices  2.46 us (5%)
    all_to_all x1, blocking collectives, on_device(): got = lax.all_to_all(packed.reshape(count, ROWS, 1, lanes), GY, 0, 0)  23.2 us
    all_to_all x1, blocking collectives, on_device(): back = lax.all_to_all(out, GY, 0, 0)  15.5 us
    pallas_call x1, Pallas kernels, on_device(): pl.pallas_call(forward, out_shape=(vmem(rows, nf, span, lanes), vmem(nf,...  2.86 us
    ppermute x1, starting transfers between devices, on_device(): outer = lax.ppermute(outer, GZ, both(pairs(around, 1) + [(around - 1, 0)]))  2.37 us
    pallas_call x1, Pallas kernels, on_device(): pl.pallas_call(finish, out_shape=shape(rows, nf, span, lanes), in_specs=[...  2.25 us
    pallas_call x1, Pallas kernels, on_device(): pl.pallas_call(collect, out_shape=(vmem(rows, span, lanes), vmem(3, rows,...  1.63 us
  transfers between devices with their start and end apart: 2, of which 0 were waited for; matrix products, arithmetic and copies ran while one was open for 0% of the time, Pallas kernels for 7%

profile of v3, /device:TPU:2, one launch (start us, length us, event | category | flops | bytes accessed | tf_op | source)
XLA Modules:
  0.0 49.3 jit_solution(3382605636297127636)
XLA Ops:
  0.0 0.0 copy-start
  0.0 1.6 %collect.1 = (f32[64,32,128]{2,1,0:T(8,128)S(1)}, f32[3,64,8,128]{3,2,1,0:T(8,128)S(1)}, f32[64,4,1,128]{3,2,1,0:T(1,128)S(1)}, f32[64,4,1,128]{3,2,1,0:T(1,128)S(1)}) custom-call(s32[1]{0:T(128)} %bitcast.side, f32[64,4,32,128]{3,2,1,0:T(8,128)} %fields.3, f32[64,32,128]{2,1,0:T(8,128)} %kappa.1, f32[4,64]{1,0:T(4,128)} %bitcast.10, f32[4,64]{1,0:T(4,128)} %bitcast.11, ...), custom_call_target="tpu_custom_call" | custom-call | tf_op jit(solution)/shard_map/collect/pallas_call | solution.py:304
  1.6 0.1 collective-permute-start
  1.7 2.4 %collective-permute-start.1 = (f32[64,4,1,128]{3,2,1,0:T(1,128)S(1)}, f32[64,4,1,128]{3,2,1,0:T(1,128)S(1)}, u32[]{:S(2)}, u32[]{:S(2)}) collective-permute-start(f32[64,4,1,128]{3,2,1,0:T(1,128)S(1)} %get-tuple-element.27), channel_id=1, source_target_pairs={{1,2},{3,4},{5,6},{7,0},{2,1},{4,3},{6,5},{0,7},{9,10},{11,12},{13... | collective-permute-start | bytes 393224 | tf_op jit(solution)/shard_map/ppermute | solution.py:318
  4.1 0.0 copy-done
  4.1 2.9 %forward.1 = (f32[64,4,32,128]{3,2,1,0:T(8,128)S(1)}, f32[4,32,128]{2,1,0:T(8,128)S(1)}, f32[2,4,32,128]{3,2,1,0:T(8,128)S(1)}) custom-call(f32[64,4,32,128]{3,2,1,0:T(8,128)S(1)} %copy-done, f32[64,32,128]{2,1,0:T(8,128)S(1)} %get-tuple-element.21.weight.kappa, f32[3,64,8,128]{3,2,1,0:T(8,128)S(1)} %get-tuple-element.20.wide), custom_call_target="tpu_custom_call" | custom-call | flops 20971520 | bytes 4194304 | tf_op jit(solution)/shard_map/forward/pallas_call | solution.py:321
  7.0 0.6 %backward.1 = (f32[64,4,32,128]{3,2,1,0:T(8,128)S(1)}, f32[4,32,128]{2,1,0:T(8,128)S(1)}) custom-call(f32[3,64,8,128]{3,2,1,0:T(8,128)S(1)} %get-tuple-element.20.wide, f32[64,4,32,128]{3,2,1,0:T(8,128)S(1)} %get-tuple-element.22.sweep), custom_call_target="tpu_custom_call", output_to_operand_aliasing={{0}: (1, {})} | custom-call | flops 1 | bytes 1 | tf_op jit(solution)/shard_map/backward/pallas_call | solution.py:331
  7.6 0.0 collective-permute-done.inner
  7.6 0.0 collective-permute-done.1.outer
  7.6 0.4 edges.1
  8.0 23.2 %all_to_all.10 = f32[32,19,1,128]{3,2,1,0:T(1,128)S(1)} all-to-all(f32[32,19,1,128]{3,2,1,0:T(1,128)S(1)} %bitcast.9), channel_id=1, replica_groups=mesh['y'=4,'z'=8,'x'=4,'c'=2] {'y','z'}, dimensions={0} | all-to-all | bytes 622592 | tf_op jit(solution)/shard_map/all_to_all | solution.py:357
  31.2 0.3 solve.1
  31.5 15.5 %all_to_all.11 = f32[32,8,128]{2,1,0:T(8,128)S(1)} all-to-all(f32[32,8,128]{2,1,0:T(8,128)S(1)} %get-tuple-element.32), channel_id=1, replica_groups=mesh['y'=4,'z'=8,'x'=4,'c'=2] {'y','z'}, dimensions={0} | all-to-all | bytes 262144 | tf_op jit(solution)/shard_map/all_to_all | solution.py:368
  47.0 2.3 %finish.1 = f32[64,4,32,128]{3,2,1,0:T(8,128)} custom-call(f32[64,4,32,128]{3,2,1,0:T(8,128)S(1)} %get-tuple-element.31.base, f32[256,128]{1,0:T(8,128)S(1)} %bitcast.8, f32[64,8,128]{2,1,0:T(8,128)S(1)} %get-tuple-element.33.resp, f32[64,8,128]{2,1,0:T(8,128)S(1)} %get-tuple-element.34.fix), custom_call_target="tpu_custom_call" | custom-call | tf_op jit(solution)/shard_map/finish/pallas_call | solution.py:369
Async XLA Ops:
  0.0 4.1 %copy-start = (f32[64,4,32,128]{3,2,1,0:T(8,128)S(1)}, f32[64,4,32,128]{3,2,1,0:T(8,128)}, u32[]{:S(2)}) copy-start(f32[64,4,32,128]{3,2,1,0:T(8,128)} %fields.3) | copy-start | bytes 12582916
  1.6 5.9 %collective-permute-start = (f32[64,4,1,128]{3,2,1,0:T(1,128)S(1)}, f32[64,4,1,128]{3,2,1,0:T(1,128)S(1)}, u32[]{:S(2)}, u32[]{:S(2)}) collective-permute-start(f32[64,4,1,128]{3,2,1,0:T(1,128)S(1)} %get-tuple-element.26), channel_id=1, source_target_pairs={{0,1},{2,3},{4,5},{6,7},{1,0},{3,2},{5,4},{7,6},{8,9},{10,11},{12,... | collective-permute-start | bytes 393224 | tf_op jit(solution)/shard_map/ppermute | solution.py:319
  1.7 5.8 %collective-permute-start.1 = (f32[64,4,1,128]{3,2,1,0:T(1,128)S(1)}, f32[64,4,1,128]{3,2,1,0:T(1,128)S(1)}, u32[]{:S(2)}, u32[]{:S(2)}) collective-permute-start(f32[64,4,1,128]{3,2,1,0:T(1,128)S(1)} %get-tuple-element.27), channel_id=1, source_target_pairs={{1,2},{3,4},{5,6},{7,0},{2,1},{4,3},{6,5},{0,7},{9,10},{11,12},{13... | collective-permute-start | bytes 393224 | tf_op jit(solution)/shard_map/ppermute | solution.py:318

commit v4 on v3

--- a/solution.py
+++ b/solution.py
@@ -11,7 +11,7 @@
 FIELDS = 4
 TILE = 8
 STEP = 8
-ROWS = 4 * FIELDS + 3
+ROWS = 3 * FIELDS + 2
 
 VMEM = pl.BlockSpec(memory_space=pltpu.VMEM)
 SMEM = pl.BlockSpec(memory_space=pltpu.SMEM)
@@ -27,15 +27,16 @@
     return lax.broadcasted_iota(jnp.int32, shape, 1)
 
 
-def collect(side, fields, kappa, fwd, piv, bwd, weight, wide, inner, outer, narrow, sems):
+def collect(side, odd, fields, kappa, fwd, piv, bwd, weight, wide, inner, outer, near, narrow, sems):
     rows, _, span, lanes = fields.shape
     z_near = jnp.where(side[0] == 0, span - 1, 0)
     copies = [
         pltpu.make_async_copy(fields.at[:, :, pl.ds(span - 1 - z_near, 1)], outer, sems.at[0]),
         pltpu.make_async_copy(fields.at[:, :, pl.ds(z_near, 1)], inner, sems.at[1]),
-        pltpu.make_async_copy(kappa, weight, sems.at[2]),
+        pltpu.make_async_copy(fields.at[jnp.where(odd[0] == 0, rows - 1, 0)], near, sems.at[2]),
+        pltpu.make_async_copy(kappa, weight, sems.at[3]),
     ]
-    small = [pltpu.make_async_copy(ref, narrow.at[i], sems.at[3 + i]) for i, ref in enumerate((fwd, piv, bwd))]
+    small = [pltpu.make_async_copy(ref, narrow.at[i], sems.at[4 + i]) for i, ref in enumerate((fwd, piv, bwd))]
     for copy in small + copies:
         copy.start()
     for copy in small:
@@ -143,7 +144,7 @@
             first[f, at(v)] = state[f * tiles + v]
 
 
-def edges(side, base_in, last, first, kappa, inner, outer, layers, wide, base, fix, packed, resp):
+def edges(side, odd, base_in, last, first, kappa, inner, outer, near, layers, wide, base, fix, packed, resp, entry):
     del base_in, base
     nf, span, lanes = last.shape
     rows = fix.shape[0]
@@ -153,6 +154,7 @@
     low, high = sub == 0, sub == TILE - 1
     upper = sub < FIELDS
     flip = jnp.broadcast_to(side[0], tile) == 1
+    even = jnp.broadcast_to(odd[0], tile) == 0
     zero, one = jnp.zeros(tile, f32), jnp.ones(tile, f32)
     twice = lambda x: jnp.concatenate([x, x], axis=0)
 
@@ -176,11 +178,18 @@
             r = r * m
         resp[j] = jnp.where(upper, a, r)
 
+    lift = wide[1, rows - 1]
+    by_value, by_answer = jnp.where(even, one, q), jnp.where(even, r * lift, a)
     for v in range(tiles):
         here = pl.ds(v * TILE, TILE)
         put = lambda i, x: packed.__setitem__(pl.ds(v * TILE * ROWS + i, TILE, stride=ROWS), x)
+        bottom, roof = kappa[0, here], kappa[rows - 1, here]
         for f in range(FIELDS):
-            value, answer = last[f, here], first[f, here]
+            brought = jnp.where(even, roof, bottom) * near[f, here]
+            entry[0, f, here] = jnp.where(even, 0.0, brought)
+            entry[1, f, here] = jnp.where(even, lift[f : f + 1] * brought, 0.0)
+            value = last[f, here] + by_value[f : f + 1] * brought
+            answer = first[f, here] + by_answer[f : f + 1] * brought
             if v == 0:
                 value = value + jnp.where(low, state[f : f + 1], 0.0)
                 answer = answer + jnp.where(low, top[f : f + 1], 0.0)
@@ -189,11 +198,9 @@
                 answer = answer + jnp.where(high, top[FIELDS + f : FIELDS + f + 1], 0.0)
             put(f, value)
             put(FIELDS + f, answer)
-            put(2 * FIELDS + f, layers[0, f, here])
-            put(3 * FIELDS + f, layers[1, f, here])
-        put(4 * FIELDS, kappa[0, here])
-        put(4 * FIELDS + 1, kappa[rows - 1, here])
-    enters, leaves, lift = wide[0, 0], wide[2, rows - 1], wide[1, rows - 1]
+            put(2 * FIELDS + f, jnp.where(even, layers[1, f, here], layers[0, f, here]))
+        put(3 * FIELDS, jnp.where(even, bottom, roof))
+    enters, leaves = wide[0, 0], wide[2, rows - 1]
     coefs = (
         jnp.where(upper, q, r * lift),
         jnp.where(upper, one, a),
@@ -225,13 +232,14 @@
         row = jnp.where(lane == i * TILE + sub, row, 0.0)
         return jnp.broadcast_to(jnp.sum(row, axis=1, keepdims=True), tile)
 
-    def layer(k):
-        return got[pl.ds(k * ROWS + 2 * FIELDS, TILE)] if 0 <= k < count else zero
-
+    twice = lambda x: jnp.concatenate([x, x], axis=0)
     e = zero
     for k in range(count):
-        weight = jnp.where(upper, got[pl.ds(k * ROWS + 4 * FIELDS, 1)], got[pl.ds(k * ROWS + 4 * FIELDS + 1, 1)])
-        brought = weight * jnp.where(upper, layer(k - 1), layer(k + 1))
+        other = k + 1 if k % 2 else k - 1
+        brought = zero
+        if 0 <= other < count:
+            layer = twice(got[pl.ds(other * ROWS + 2 * FIELDS, FIELDS)])
+            brought = jnp.where(upper == (k % 2 == 0), got[pl.ds(k * ROWS + 3 * FIELDS, 1)] * layer, 0.0)
         both = got[pl.ds(k * ROWS, TILE)] + coefficient(k, 0) * brought + coefficient(k, 1) * swap(brought)
         entry[0, k] = both
         entry[1, k] = coefficient(k, 6) * brought
@@ -244,7 +252,7 @@
         b = jnp.where(upper, swap(both), both) + coefficient(k, 3) * e + coefficient(k, 4) * b
 
 
-def finish(base, got, resp, fix, out, start, stage, sems):
+def finish(base, got, entry, resp, fix, out, start, stage, sems):
     rows, _, span, lanes = out.shape
     tiles = span // TILE
     sub = row_of((TILE, lanes))
@@ -257,8 +265,8 @@
     for f in range(FIELDS):
         for v in range(tiles):
             here = pl.ds(v * TILE, TILE)
-            start[0, f, here] = got[pl.ds(v * TILE * TILE + f, TILE, stride=TILE)]
-            start[1, f, here] = got[pl.ds(v * TILE * TILE + FIELDS + f, TILE, stride=TILE)]
+            start[0, f, here] = got[pl.ds(v * TILE * TILE + f, TILE, stride=TILE)] + entry[0, f, here]
+            start[1, f, here] = got[pl.ds(v * TILE * TILE + FIELDS + f, TILE, stride=TILE)] + entry[1, f, here]
 
     def body(c, carry):
         for f in range(FIELDS):
@@ -298,24 +306,27 @@
     pairs = lambda n, first: [(i, i + 1) for i in range(first, n - 1, 2)]
     both = lambda ends: ends + [(b, a) for a, b in ends]
     side = lax.axis_index("c").astype(jnp.int32).reshape(1)
+    odd = (lax.axis_index("z") & 1).astype(jnp.int32).reshape(1)
     fwd, piv, bwd = fwd.T, piv.T, bwd.T
     fields, kappa = in_hbm(fields), in_hbm(kappa)
     chunks = rows // STEP
-    weight, wide, inner, outer = pl.pallas_call(
+    weight, wide, inner, outer, near = pl.pallas_call(
         collect,
         out_shape=(
             vmem(rows, span, lanes),
             vmem(3, rows, TILE, lanes),
             vmem(rows, nf, 1, lanes),
             vmem(rows, nf, 1, lanes),
+            vmem(nf, span, lanes),
         ),
-        in_specs=[SMEM] + [HBM] * 5,
-        out_specs=(VMEM,) * 4,
-        scratch_shapes=[pltpu.VMEM((3, nf, rows), f32), pltpu.SemaphoreType.DMA((6,))],
+        in_specs=[SMEM, SMEM] + [HBM] * 5,
+        out_specs=(VMEM,) * 5,
+        scratch_shapes=[pltpu.VMEM((3, nf, rows), f32), pltpu.SemaphoreType.DMA((7,))],
         compiler_params=params(4),
         name="collect",
-    )(side, *map(in_hbm, (fields, kappa, fwd, piv, bwd)))
+    )(side, odd, *map(in_hbm, (fields, kappa, fwd, piv, bwd)))
     outer = lax.ppermute(outer, GZ, both(pairs(around, 1) + [(around - 1, 0)]))
+    near = lax.ppermute(near, GY, both(pairs(count, 0)))
     inner = lax.ppermute(inner, GZ, both(pairs(around, 0)))
     block = in_vmem(fields), in_vmem(weight), in_vmem(wide)
     sweep, last, layers = pl.pallas_call(
@@ -339,20 +350,21 @@
         name="backward",
     )(in_vmem(wide), in_vmem(sweep))
 
-    base, fix, packed, resp = pl.pallas_call(
+    base, fix, packed, resp, entry = pl.pallas_call(
         edges,
         out_shape=(
             vmem(rows, nf, span, lanes),
             shape(rows, TILE, lanes),
             shape(span * ROWS, lanes),
             shape(rows, TILE, lanes),
+            shape(2, nf, span, lanes),
         ),
-        in_specs=[SMEM] + [VMEM] * 8,
-        out_specs=(VMEM,) * 4,
-        input_output_aliases={1: 0},
+        in_specs=[SMEM, SMEM] + [VMEM] * 9,
+        out_specs=(VMEM,) * 5,
+        input_output_aliases={2: 0},
         compiler_params=params(4),
         name="edges",
-    )(side, in_vmem(base), last, first, in_vmem(weight), inner, outer, layers, in_vmem(wide))
+    )(side, odd, in_vmem(base), last, first, in_vmem(weight), inner, outer, near, layers, in_vmem(wide))
 
     got = lax.all_to_all(packed.reshape(count, ROWS, 1, lanes), GY, 0, 0)
     out, base = pl.pallas_call(
@@ -369,7 +381,7 @@
     return pl.pallas_call(
         finish,
         out_shape=shape(rows, nf, span, lanes),
-        in_specs=[VMEM] * 4,
+        in_specs=[VMEM] * 5,
         out_specs=HBM,
         scratch_shapes=[
             pltpu.VMEM((2, nf, span, lanes), f32),
@@ -378,7 +390,7 @@
         ],
         compiler_params=params(16),
         name="finish",
-    )(in_vmem(base), back.reshape(count * TILE, lanes), resp, fix)
+    )(in_vmem(base), back.reshape(count * TILE, lanes), entry, resp, fix)
 
 
 def solution(mesh):

time: 49.9 us -> 48.7 us (0.976)
  blocking collectives: 38.8 us -> 37 us
  waiting for transfers between devices: 0.01 us -> 0.7 us
    all_to_all x1, blocking collectives: 15.5 us -> 14.3 us  [on_device(): back = lax.all_to_all(out, GY, 0, 0)]
    ppermute x0 -> x1, waiting for transfers between devices: none -> 0.7 us  [on_device(): near = lax.ppermute(near, GY, both(pairs(count, 0)))]
    all_to_all x1, blocking collectives: 23.2 us -> 22.6 us  [on_device(): got = lax.all_to_all(packed.reshape(count, ROWS, 1, lanes), GY, 0, 0)]
  transfers between devices with their start and end apart: 2 -> 3, of which waited for: 0 -> 1; matrix products, arithmetic and copies ran while one was open for 0% -> 0% of each run, Pallas kernels for 7% -> 7%
where the time goes in v4:
time: 48.7 us; the launch traced here: 48.3 us
  blocking collectives  37 us (76%)
  Pallas kernels  7.97 us (16%)
  starting transfers between devices  2.65 us (5%)
  waiting for transfers between devices  0.7 us (1%)
    all_to_all x1, blocking collectives, on_device(): got = lax.all_to_all(packed.reshape(count, ROWS, 1, lanes), GY, 0, 0)  22.6 us
    all_to_all x1, blocking collectives, on_device(): back = lax.all_to_all(out, GY, 0, 0)  14.3 us
    pallas_call x1, Pallas kernels, on_device(): pl.pallas_call(forward, out_shape=(vmem(rows, nf, span, lanes), vmem(nf,...  2.8 us
    ppermute x1, starting transfers between devices, on_device(): outer = lax.ppermute(outer, GZ, both(pairs(around, 1) + [(around - 1, 0)]))  2.37 us
    pallas_call x1, Pallas kernels, on_device(): pl.pallas_call(finish, out_shape=shape(rows, nf, span, lanes), in_specs=[...  2.26 us
    pallas_call x1, Pallas kernels, on_device(): pl.pallas_call(collect, out_shape=(vmem(rows, span, lanes), vmem(3, rows,...  1.67 us
  transfers between devices with their start and end apart: 3, of which 1 were waited for; matrix products, arithmetic and copies ran while one was open for 0% of the time, Pallas kernels for 7%

profile of v4, /device:TPU:2, one launch (start us, length us, event | category | flops | bytes accessed | tf_op | source)
XLA Modules:
  0.0 48.3 jit_solution(13262904525651657438)
XLA Ops:
  0.0 0.0 copy-start
  0.0 1.7 %collect.1 = (f32[64,32,128]{2,1,0:T(8,128)S(1)}, f32[3,64,8,128]{3,2,1,0:T(8,128)S(1)}, f32[64,4,1,128]{3,2,1,0:T(1,128)S(1)}, f32[64,4,1,128]{3,2,1,0:T(1,128)S(1)}, f32[4,32,128]{2,1,0:T(8,128)S(1)}) custom-call(s32[1]{0:T(128)} %bitcast.side, s32[1]{0:T(128)} %bitcast.1.odd, f32[64,4,32,128]{3,2,1,0:T(8,128)} %fields.3, f32[64,32,128]{2,1,0:T(8,128)} %kappa.1, ...), custom_call_target="tpu_custom_call" | custom-call | tf_op jit(solution)/shard_map/collect/pallas_call | solution.py:313
  1.7 0.1 collective-permute-start
  1.8 2.4 %collective-permute-start.1 = (f32[64,4,1,128]{3,2,1,0:T(1,128)S(1)}, f32[64,4,1,128]{3,2,1,0:T(1,128)S(1)}, u32[]{:S(2)}, u32[]{:S(2)}) collective-permute-start(f32[64,4,1,128]{3,2,1,0:T(1,128)S(1)} %get-tuple-element.29), channel_id=1, source_target_pairs={{1,2},{3,4},{5,6},{7,0},{2,1},{4,3},{6,5},{0,7},{9,10},{11,12},{13... | collective-permute-start | bytes 393224 | tf_op jit(solution)/shard_map/ppermute | solution.py:328
  4.2 0.2 collective-permute-start.2
  4.3 0.0 copy-done
  4.3 2.8 %forward.1 = (f32[64,4,32,128]{3,2,1,0:T(8,128)S(1)}, f32[4,32,128]{2,1,0:T(8,128)S(1)}, f32[2,4,32,128]{3,2,1,0:T(8,128)S(1)}) custom-call(f32[64,4,32,128]{3,2,1,0:T(8,128)S(1)} %copy-done, f32[64,32,128]{2,1,0:T(8,128)S(1)} %get-tuple-element.23.weight.kappa, f32[3,64,8,128]{3,2,1,0:T(8,128)S(1)} %get-tuple-element.22.wide), custom_call_target="tpu_custom_call" | custom-call | flops 20971520 | bytes 4194304 | tf_op jit(solution)/shard_map/forward/pallas_call | solution.py:332
  7.1 0.6 %backward.1 = (f32[64,4,32,128]{3,2,1,0:T(8,128)S(1)}, f32[4,32,128]{2,1,0:T(8,128)S(1)}) custom-call(f32[3,64,8,128]{3,2,1,0:T(8,128)S(1)} %get-tuple-element.22.wide, f32[64,4,32,128]{3,2,1,0:T(8,128)S(1)} %get-tuple-element.24.sweep), custom_call_target="tpu_custom_call", output_to_operand_aliasing={{0}: (1, {})} | custom-call | flops 1 | bytes 1 | tf_op jit(solution)/shard_map/backward/pallas_call | solution.py:342
  7.7 0.7 %collective-permute-done.2.near = f32[4,32,128]{2,1,0:T(8,128)S(1)} collective-permute-done((f32[4,32,128]{2,1,0:T(8,128)S(1)}, f32[4,32,128]{2,1,0:T(8,128)S(1)}, u32[]{:S(2)}, u32[]{:S(2)}) %collective-permute-start.2) | collective-permute-done | bytes 65568 | tf_op jit(solution)/shard_map/ppermute | solution.py:329
  8.4 0.0 collective-permute-done.inner
  8.4 0.0 collective-permute-done.1.outer
  8.4 0.4 edges.1
  8.8 22.6 %all_to_all.10 = f32[32,14,1,128]{3,2,1,0:T(1,128)S(1)} all-to-all(f32[32,14,1,128]{3,2,1,0:T(1,128)S(1)} %bitcast.10), channel_id=1, replica_groups=mesh['y'=4,'z'=8,'x'=4,'c'=2] {'y','z'}, dimensions={0} | all-to-all | bytes 458752 | tf_op jit(solution)/shard_map/all_to_all | solution.py:369
  31.4 0.3 solve.1
  31.8 14.3 %all_to_all.11 = f32[32,8,128]{2,1,0:T(8,128)S(1)} all-to-all(f32[32,8,128]{2,1,0:T(8,128)S(1)} %get-tuple-element.35), channel_id=1, replica_groups=mesh['y'=4,'z'=8,'x'=4,'c'=2] {'y','z'}, dimensions={0} | all-to-all | bytes 262144 | tf_op jit(solution)/shard_map/all_to_all | solution.py:380
  46.1 2.3 %finish.1 = f32[64,4,32,128]{3,2,1,0:T(8,128)} custom-call(f32[64,4,32,128]{3,2,1,0:T(8,128)S(1)} %get-tuple-element.34.base, f32[256,128]{1,0:T(8,128)S(1)} %bitcast.9, f32[2,4,32,128]{3,2,1,0:T(8,128)S(1)} %get-tuple-element.36.entry, f32[64,8,128]{2,1,0:T(8,128)S(1)} %get-tuple-element.37.resp, f32[64,8,128]{2,1,0:T(8,128)S(1)} %get-tuple-element.38.fix), custom_call_target="tpu_custom_call" | custom-call | tf_op jit(solution)/shard_map/finish/pallas_call | solution.py:381
Async XLA Ops:
  0.0 4.3 %copy-start = (f32[64,4,32,128]{3,2,1,0:T(8,128)S(1)}, f32[64,4,32,128]{3,2,1,0:T(8,128)}, u32[]{:S(2)}) copy-start(f32[64,4,32,128]{3,2,1,0:T(8,128)} %fields.3) | copy-start | bytes 12582916
  1.7 6.7 %collective-permute-start = (f32[64,4,1,128]{3,2,1,0:T(1,128)S(1)}, f32[64,4,1,128]{3,2,1,0:T(1,128)S(1)}, u32[]{:S(2)}, u32[]{:S(2)}) collective-permute-start(f32[64,4,1,128]{3,2,1,0:T(1,128)S(1)} %get-tuple-element.28), channel_id=1, source_target_pairs={{0,1},{2,3},{4,5},{6,7},{1,0},{3,2},{5,4},{7,6},{8,9},{10,11},{12,... | collective-permute-start | bytes 393224 | tf_op jit(solution)/shard_map/ppermute | solution.py:330
  1.8 6.6 %collective-permute-start.1 = (f32[64,4,1,128]{3,2,1,0:T(1,128)S(1)}, f32[64,4,1,128]{3,2,1,0:T(1,128)S(1)}, u32[]{:S(2)}, u32[]{:S(2)}) collective-permute-start(f32[64,4,1,128]{3,2,1,0:T(1,128)S(1)} %get-tuple-element.29), channel_id=1, source_target_pairs={{1,2},{3,4},{5,6},{7,0},{2,1},{4,3},{6,5},{0,7},{9,10},{11,12},{13... | collective-permute-start | bytes 393224 | tf_op jit(solution)/shard_map/ppermute | solution.py:328
  4.2 4.3 %collective-permute-start.2 = (f32[4,32,128]{2,1,0:T(8,128)S(1)}, f32[4,32,128]{2,1,0:T(8,128)S(1)}, u32[]{:S(2)}, u32[]{:S(2)}) collective-permute-start(f32[4,32,128]{2,1,0:T(8,128)S(1)} %get-tuple-element.30), channel_id=1, source_target_pairs={{0,8},{16,24},{32,40},{48,56},{64,72},{80,88},{96,104},{112,120},{... | collective-permute-start | bytes 196616 | tf_op jit(solution)/shard_map/ppermute | solution.py:329

commit v5 on v4

--- a/solution.py
+++ b/solution.py
@@ -10,6 +10,7 @@
 GZ = ("x", "c")
 FIELDS = 4
 TILE = 8
+LONG = 16
 STEP = 8
 ROWS = 3 * FIELDS + 2
 
@@ -56,7 +57,7 @@
     tile = (TILE, lanes)
     at = lambda v: pl.ds(v * TILE, TILE)
     sub = row_of(tile)
-    total = rows // STEP
+    total = rows // LONG
     layers[0] = fields[rows - 1]
     layers[1] = fields[0]
 
@@ -73,16 +74,16 @@
         above_first = jnp.where(jnp.broadcast_to(c, tile) > 0, 1.0, 0.0)
         below_last = jnp.where(jnp.broadcast_to(c, tile) < total - 1, 1.0, 0.0)
         for v in range(tiles):
-            under = [fields[jnp.maximum(c * STEP - 1, 0), f, at(v)] * above_first for f in range(FIELDS)]
-            here = [fields[c * STEP, f, at(v)] for f in range(FIELDS)]
-            for i in range(STEP):
-                j = c * STEP + i
+            under = [fields[jnp.maximum(c * LONG - 1, 0), f, at(v)] * above_first for f in range(FIELDS)]
+            here = [fields[c * LONG, f, at(v)] for f in range(FIELDS)]
+            for i in range(LONG):
+                j = c * LONG + i
                 k = weight[j, at(v)]
                 own = 1.0 - 6.0 * k
                 half = 0.5 * here[0]
                 for f in range(FIELDS):
                     x = here[f]
-                    if i < STEP - 1:
+                    if i < LONG - 1:
                         over = fields[j + 1, f, at(v)]
                     else:
                         over = fields[jnp.minimum(j + 1, rows - 1), f, at(v)] * below_last
@@ -97,8 +98,8 @@
 
     def advance(c, carry):
         carry = list(carry)
-        for i in range(STEP):
-            j = c * STEP + i
+        for i in range(LONG):
+            j = c * LONG + i
             for f in range(FIELDS):
                 m = wide[0, j, pl.ds(f, 1)]
                 for v in range(tiles):
@@ -142,6 +143,11 @@
     for f in range(FIELDS):
         for v in range(tiles):
             first[f, at(v)] = state[f * tiles + v]
+
+
+def sweeps(fields, weight, wide, base, last, layers, first, fresh):
+    forward(fields, weight, wide, base, last, layers, fresh)
+    backward(wide, None, base, first)
 
 
 def edges(side, odd, base_in, last, first, kappa, inner, outer, near, layers, wide, base, fix, packed, resp, entry):
@@ -329,26 +335,21 @@
     near = lax.ppermute(near, GY, both(pairs(count, 0)))
     inner = lax.ppermute(inner, GZ, both(pairs(around, 0)))
     block = in_vmem(fields), in_vmem(weight), in_vmem(wide)
-    sweep, last, layers = pl.pallas_call(
-        forward,
-        out_shape=(vmem(rows, nf, span, lanes), vmem(nf, span, lanes), vmem(2, nf, span, lanes)),
+    base, last, layers, first = pl.pallas_call(
+        sweeps,
+        out_shape=(
+            vmem(rows, nf, span, lanes),
+            vmem(nf, span, lanes),
+            vmem(2, nf, span, lanes),
+            vmem(nf, span, lanes),
+        ),
         in_specs=[VMEM] * 3,
-        out_specs=(VMEM,) * 3,
-        scratch_shapes=[pltpu.VMEM((STEP, nf, span, lanes), f32)],
+        out_specs=(VMEM,) * 4,
+        scratch_shapes=[pltpu.VMEM((LONG, nf, span, lanes), f32)],
         compiler_params=params(4),
         cost_estimate=pl.CostEstimate(flops=20 * fields.size, bytes_accessed=4 * fields.size, transcendentals=0),
-        name="forward",
+        name="sweeps",
     )(*block)
-    base, first = pl.pallas_call(
-        backward,
-        out_shape=(vmem(rows, nf, span, lanes), vmem(nf, span, lanes)),
-        in_specs=[VMEM, VMEM],
-        out_specs=(VMEM, VMEM),
-        input_output_aliases={1: 0},
-        compiler_params=params(4),
-        cost_estimate=pl.CostEstimate(flops=1, bytes_accessed=1, transcendentals=0),
-        name="backward",
-    )(in_vmem(wide), in_vmem(sweep))
 
     base, fix, packed, resp, entry = pl.pallas_call(
         edges,

time: 48.7 us -> 48.7 us (level)
    pallas_call x2 -> x1, Pallas kernels: 3.37 us -> 3.39 us  [on_device(): pl.pallas_call(sweeps, out_shape=(vmem(rows, nf, span, lanes), vmem(nf, s...]
where the time goes in v5:
time: 48.7 us; the launch traced here: 48.4 us
  blocking collectives  37 us (76%)
  Pallas kernels  8 us (16%)
  starting transfers between devices  2.65 us (5%)
  waiting for transfers between devices  0.69 us (1%)
    all_to_all x1, blocking collectives, on_device(): got = lax.all_to_all(packed.reshape(count, ROWS, 1, lanes), GY, 0, 0)  22.6 us
    all_to_all x1, blocking collectives, on_device(): back = lax.all_to_all(out, GY, 0, 0)  14.3 us
    pallas_call x1, Pallas kernels, on_device(): pl.pallas_call(sweeps, out_shape=(vmem(rows, nf, span, lanes), vmem(nf, s...  3.39 us
    ppermute x1, starting transfers between devices, on_device(): outer = lax.ppermute(outer, GZ, both(pairs(around, 1) + [(around - 1, 0)]))  2.37 us
    pallas_call x1, Pallas kernels, on_device(): pl.pallas_call(finish, out_shape=shape(rows, nf, span, lanes), in_specs=[...  2.26 us
    pallas_call x1, Pallas kernels, on_device(): pl.pallas_call(collect, out_shape=(vmem(rows, span, lanes), vmem(3, rows,...  1.67 us
  transfers between devices with their start and end apart: 3, of which 1 were waited for; matrix products, arithmetic and copies ran while one was open for 0% of the time, Pallas kernels for 7%

profile of v5, /device:TPU:2, one launch (start us, length us, event | category | flops | bytes accessed | tf_op | source)
XLA Modules:
  0.0 48.4 jit_solution(8181065832099179632)
XLA Ops:
  0.0 0.0 copy-start
  0.0 1.7 %collect.1 = (f32[64,32,128]{2,1,0:T(8,128)S(1)}, f32[3,64,8,128]{3,2,1,0:T(8,128)S(1)}, f32[64,4,1,128]{3,2,1,0:T(1,128)S(1)}, f32[64,4,1,128]{3,2,1,0:T(1,128)S(1)}, f32[4,32,128]{2,1,0:T(8,128)S(1)}) custom-call(s32[1]{0:T(128)} %bitcast.side, s32[1]{0:T(128)} %bitcast.1.odd, f32[64,4,32,128]{3,2,1,0:T(8,128)} %fields.3, f32[64,32,128]{2,1,0:T(8,128)} %kappa.1, ...), custom_call_target="tpu_custom_call" | custom-call | tf_op jit(solution)/shard_map/collect/pallas_call | solution.py:319
  1.7 0.1 collective-permute-start
  1.8 2.4 %collective-permute-start.1 = (f32[64,4,1,128]{3,2,1,0:T(1,128)S(1)}, f32[64,4,1,128]{3,2,1,0:T(1,128)S(1)}, u32[]{:S(2)}, u32[]{:S(2)}) collective-permute-start(f32[64,4,1,128]{3,2,1,0:T(1,128)S(1)} %get-tuple-element.27), channel_id=1, source_target_pairs={{1,2},{3,4},{5,6},{7,0},{2,1},{4,3},{6,5},{0,7},{9,10},{11,12},{13... | collective-permute-start | bytes 393224 | tf_op jit(solution)/shard_map/ppermute | solution.py:334
  4.2 0.2 collective-permute-start.2
  4.3 0.0 copy-done
  4.3 3.4 %sweeps.1 = (f32[64,4,32,128]{3,2,1,0:T(8,128)S(1)}, f32[4,32,128]{2,1,0:T(8,128)S(1)}, f32[2,4,32,128]{3,2,1,0:T(8,128)S(1)}, f32[4,32,128]{2,1,0:T(8,128)S(1)}) custom-call(f32[64,4,32,128]{3,2,1,0:T(8,128)S(1)} %copy-done, f32[64,32,128]{2,1,0:T(8,128)S(1)} %get-tuple-element.21.weight.kappa, f32[3,64,8,128]{3,2,1,0:T(8,128)S(1)} %get-tuple-element.22.wide), custom_call_target="tpu_custom_call" | custom-call | flops 20971520 | bytes 4194304 | tf_op jit(solution)/shard_map/sweeps/pallas_call | solution.py:338
  7.7 0.7 %collective-permute-done.2.near = f32[4,32,128]{2,1,0:T(8,128)S(1)} collective-permute-done((f32[4,32,128]{2,1,0:T(8,128)S(1)}, f32[4,32,128]{2,1,0:T(8,128)S(1)}, u32[]{:S(2)}, u32[]{:S(2)}) %collective-permute-start.2) | collective-permute-done | bytes 65568 | tf_op jit(solution)/shard_map/ppermute | solution.py:335
  8.4 0.0 collective-permute-done.inner
  8.4 0.0 collective-permute-done.1.outer
  8.4 0.4 edges.1
  8.8 22.6 %all_to_all.10 = f32[32,14,1,128]{3,2,1,0:T(1,128)S(1)} all-to-all(f32[32,14,1,128]{3,2,1,0:T(1,128)S(1)} %bitcast.10), channel_id=1, replica_groups=mesh['y'=4,'z'=8,'x'=4,'c'=2] {'y','z'}, dimensions={0} | all-to-all | bytes 458752 | tf_op jit(solution)/shard_map/all_to_all | solution.py:370
  31.4 0.3 solve.1
  31.8 14.3 %all_to_all.11 = f32[32,8,128]{2,1,0:T(8,128)S(1)} all-to-all(f32[32,8,128]{2,1,0:T(8,128)S(1)} %get-tuple-element.33), channel_id=1, replica_groups=mesh['y'=4,'z'=8,'x'=4,'c'=2] {'y','z'}, dimensions={0} | all-to-all | bytes 262144 | tf_op jit(solution)/shard_map/all_to_all | solution.py:381
  46.1 2.3 %finish.1 = f32[64,4,32,128]{3,2,1,0:T(8,128)} custom-call(f32[64,4,32,128]{3,2,1,0:T(8,128)S(1)} %get-tuple-element.32.base, f32[256,128]{1,0:T(8,128)S(1)} %bitcast.9, f32[2,4,32,128]{3,2,1,0:T(8,128)S(1)} %get-tuple-element.34.entry, f32[64,8,128]{2,1,0:T(8,128)S(1)} %get-tuple-element.35.resp, f32[64,8,128]{2,1,0:T(8,128)S(1)} %get-tuple-element.36.fix), custom_call_target="tpu_custom_call" | custom-call | tf_op jit(solution)/shard_map/finish/pallas_call | solution.py:382
Async XLA Ops:
  0.0 4.3 %copy-start = (f32[64,4,32,128]{3,2,1,0:T(8,128)S(1)}, f32[64,4,32,128]{3,2,1,0:T(8,128)}, u32[]{:S(2)}) copy-start(f32[64,4,32,128]{3,2,1,0:T(8,128)} %fields.3) | copy-start | bytes 12582916
  1.7 6.7 %collective-permute-start = (f32[64,4,1,128]{3,2,1,0:T(1,128)S(1)}, f32[64,4,1,128]{3,2,1,0:T(1,128)S(1)}, u32[]{:S(2)}, u32[]{:S(2)}) collective-permute-start(f32[64,4,1,128]{3,2,1,0:T(1,128)S(1)} %get-tuple-element.26), channel_id=1, source_target_pairs={{0,1},{2,3},{4,5},{6,7},{1,0},{3,2},{5,4},{7,6},{8,9},{10,11},{12,... | collective-permute-start | bytes 393224 | tf_op jit(solution)/shard_map/ppermute | solution.py:336
  1.8 6.6 %collective-permute-start.1 = (f32[64,4,1,128]{3,2,1,0:T(1,128)S(1)}, f32[64,4,1,128]{3,2,1,0:T(1,128)S(1)}, u32[]{:S(2)}, u32[]{:S(2)}) collective-permute-start(f32[64,4,1,128]{3,2,1,0:T(1,128)S(1)} %get-tuple-element.27), channel_id=1, source_target_pairs={{1,2},{3,4},{5,6},{7,0},{2,1},{4,3},{6,5},{0,7},{9,10},{11,12},{13... | collective-permute-start | bytes 393224 | tf_op jit(solution)/shard_map/ppermute | solution.py:334
  4.2 4.3 %collective-permute-start.2 = (f32[4,32,128]{2,1,0:T(8,128)S(1)}, f32[4,32,128]{2,1,0:T(8,128)S(1)}, u32[]{:S(2)}, u32[]{:S(2)}) collective-permute-start(f32[4,32,128]{2,1,0:T(8,128)S(1)} %get-tuple-element.28), channel_id=1, source_target_pairs={{0,8},{16,24},{32,40},{48,56},{64,72},{80,88},{96,104},{112,120},{... | collective-permute-start | bytes 196616 | tf_op jit(solution)/shard_map/ppermute | solution.py:335

commit v6 on v5

--- a/solution.py
+++ b/solution.py
@@ -164,25 +164,32 @@
     zero, one = jnp.zeros(tile, f32), jnp.ones(tile, f32)
     twice = lambda x: jnp.concatenate([x, x], axis=0)
 
+    def added(j):
+        x = jnp.where(upper == flip, twice(inner[j, :, 0]), twice(outer[j, :, 0]))
+        return jnp.where(upper, kappa[j, pl.ds(0, 1)], kappa[j, pl.ds(span - 1, 1)]) * x
+
     state, q = zero, one
-    for j in range(rows):
-        x = jnp.where(upper == flip, twice(inner[j, :, 0]), twice(outer[j, :, 0]))
-        k = jnp.where(upper, kappa[j, pl.ds(0, 1)], kappa[j, pl.ds(span - 1, 1)])
-        m = wide[0, j]
-        state = k * x + m * state
-        fix[j] = state
-        if j:
-            q = q * m
-        resp[j] = q
+    for j in range(0, rows, 2):
+        x0, x1, m0, m1 = added(j), added(j + 1), wide[0, j], wide[0, j + 1]
+        fix[j] = x0 + m0 * state
+        state = (x1 + m1 * x0) + (m1 * m0) * state
+        fix[j + 1] = state
+        n0 = m0 if j else one
+        resp[j] = n0 * q
+        q = (m1 * n0) * q
+        resp[j + 1] = q
     top, a, r = zero, zero, one
-    for j in reversed(range(rows)):
-        p, m = wide[1, j], wide[2, j]
-        top = p * fix[j] + m * top
-        fix[j] = top
-        a = p * resp[j] + m * a
-        if j < rows - 1:
-            r = r * m
-        resp[j] = jnp.where(upper, a, r)
+    for j in reversed(range(1, rows, 2)):
+        p1, m1, p0, m0 = wide[1, j], wide[2, j], wide[1, j - 1], wide[2, j - 1]
+        f1, f0, a1, a0 = p1 * fix[j], p0 * fix[j - 1], p1 * resp[j], p0 * resp[j - 1]
+        fix[j] = f1 + m1 * top
+        top = (f0 + m0 * f1) + (m0 * m1) * top
+        fix[j - 1] = top
+        n1 = m1 if j < rows - 1 else one
+        resp[j] = jnp.where(upper, a1 + m1 * a, n1 * r)
+        a = (a0 + m0 * a1) + (m0 * m1) * a
+        r = (m0 * n1) * r
+        resp[j - 1] = jnp.where(upper, a, r)
 
     lift = wide[1, rows - 1]
     by_value, by_answer = jnp.where(even, one, q), jnp.where(even, r * lift, a)

time: 48.7 us -> 48.7 us (level)
  no operation moved by 1% of the time
where the time goes in v6:
time: 48.7 us; the launch traced here: 48.3 us
  blocking collectives  37 us (76%)
  Pallas kernels  7.98 us (16%)
  starting transfers between devices  2.65 us (5%)
  waiting for transfers between devices  0.69 us (1%)
    all_to_all x1, blocking collectives, on_device(): got = lax.all_to_all(packed.reshape(count, ROWS, 1, lanes), GY, 0, 0)  22.6 us
    all_to_all x1, blocking collectives, on_device(): back = lax.all_to_all(out, GY, 0, 0)  14.3 us
    pallas_call x1, Pallas kernels, on_device(): pl.pallas_call(sweeps, out_shape=(vmem(rows, nf, span, lanes), vmem(nf, s...  3.39 us
    ppermute x1, starting transfers between devices, on_device(): outer = lax.ppermute(outer, GZ, both(pairs(around, 1) + [(around - 1, 0)]))  2.37 us
    pallas_call x1, Pallas kernels, on_device(): pl.pallas_call(finish, out_shape=shape(rows, nf, span, lanes), in_specs=[...  2.26 us
    pallas_call x1, Pallas kernels, on_device(): pl.pallas_call(collect, out_shape=(vmem(rows, span, lanes), vmem(3, rows,...  1.67 us
  transfers between devices with their start and end apart: 3, of which 1 were waited for; matrix products, arithmetic and copies ran while one was open for 0% of the time, Pallas kernels for 7%

profile of v6, /device:TPU:2, one launch (start us, length us, event | category | flops | bytes accessed | tf_op | source)
XLA Modules:
  0.0 48.3 jit_solution(12571096541387885534)
XLA Ops:
  0.0 0.0 copy-start
  0.0 1.7 %collect.1 = (f32[64,32,128]{2,1,0:T(8,128)S(1)}, f32[3,64,8,128]{3,2,1,0:T(8,128)S(1)}, f32[64,4,1,128]{3,2,1,0:T(1,128)S(1)}, f32[64,4,1,128]{3,2,1,0:T(1,128)S(1)}, f32[4,32,128]{2,1,0:T(8,128)S(1)}) custom-call(s32[1]{0:T(128)} %bitcast.side, s32[1]{0:T(128)} %bitcast.1.odd, f32[64,4,32,128]{3,2,1,0:T(8,128)} %fields.3, f32[64,32,128]{2,1,0:T(8,128)} %kappa.1, ...), custom_call_target="tpu_custom_call" | custom-call | tf_op jit(solution)/shard_map/collect/pallas_call | solution.py:326
  1.7 0.1 collective-permute-start
  1.8 2.4 %collective-permute-start.1 = (f32[64,4,1,128]{3,2,1,0:T(1,128)S(1)}, f32[64,4,1,128]{3,2,1,0:T(1,128)S(1)}, u32[]{:S(2)}, u32[]{:S(2)}) collective-permute-start(f32[64,4,1,128]{3,2,1,0:T(1,128)S(1)} %get-tuple-element.27), channel_id=1, source_target_pairs={{1,2},{3,4},{5,6},{7,0},{2,1},{4,3},{6,5},{0,7},{9,10},{11,12},{13... | collective-permute-start | bytes 393224 | tf_op jit(solution)/shard_map/ppermute | solution.py:341
  4.2 0.2 collective-permute-start.2
  4.3 0.0 copy-done
  4.3 3.4 %sweeps.1 = (f32[64,4,32,128]{3,2,1,0:T(8,128)S(1)}, f32[4,32,128]{2,1,0:T(8,128)S(1)}, f32[2,4,32,128]{3,2,1,0:T(8,128)S(1)}, f32[4,32,128]{2,1,0:T(8,128)S(1)}) custom-call(f32[64,4,32,128]{3,2,1,0:T(8,128)S(1)} %copy-done, f32[64,32,128]{2,1,0:T(8,128)S(1)} %get-tuple-element.21.weight.kappa, f32[3,64,8,128]{3,2,1,0:T(8,128)S(1)} %get-tuple-element.22.wide), custom_call_target="tpu_custom_call" | custom-call | flops 20971520 | bytes 4194304 | tf_op jit(solution)/shard_map/sweeps/pallas_call | solution.py:345
  7.7 0.7 %collective-permute-done.2.near = f32[4,32,128]{2,1,0:T(8,128)S(1)} collective-permute-done((f32[4,32,128]{2,1,0:T(8,128)S(1)}, f32[4,32,128]{2,1,0:T(8,128)S(1)}, u32[]{:S(2)}, u32[]{:S(2)}) %collective-permute-start.2) | collective-permute-done | bytes 65568 | tf_op jit(solution)/shard_map/ppermute | solution.py:342
  8.4 0.0 collective-permute-done.inner
  8.4 0.0 collective-permute-done.1.outer
  8.4 0.3 edges.1
  8.8 22.6 %all_to_all.10 = f32[32,14,1,128]{3,2,1,0:T(1,128)S(1)} all-to-all(f32[32,14,1,128]{3,2,1,0:T(1,128)S(1)} %bitcast.10), channel_id=1, replica_groups=mesh['y'=4,'z'=8,'x'=4,'c'=2] {'y','z'}, dimensions={0} | all-to-all | bytes 458752 | tf_op jit(solution)/shard_map/all_to_all | solution.py:377
  31.4 0.3 solve.1
  31.7 14.3 %all_to_all.11 = f32[32,8,128]{2,1,0:T(8,128)S(1)} all-to-all(f32[32,8,128]{2,1,0:T(8,128)S(1)} %get-tuple-element.33), channel_id=1, replica_groups=mesh['y'=4,'z'=8,'x'=4,'c'=2] {'y','z'}, dimensions={0} | all-to-all | bytes 262144 | tf_op jit(solution)/shard_map/all_to_all | solution.py:388
  46.1 2.3 %finish.1 = f32[64,4,32,128]{3,2,1,0:T(8,128)} custom-call(f32[64,4,32,128]{3,2,1,0:T(8,128)S(1)} %get-tuple-element.32.base, f32[256,128]{1,0:T(8,128)S(1)} %bitcast.9, f32[2,4,32,128]{3,2,1,0:T(8,128)S(1)} %get-tuple-element.34.entry, f32[64,8,128]{2,1,0:T(8,128)S(1)} %get-tuple-element.35.resp, f32[64,8,128]{2,1,0:T(8,128)S(1)} %get-tuple-element.36.fix), custom_call_target="tpu_custom_call" | custom-call | tf_op jit(solution)/shard_map/finish/pallas_call | solution.py:389
Async XLA Ops:
  0.0 4.3 %copy-start = (f32[64,4,32,128]{3,2,1,0:T(8,128)S(1)}, f32[64,4,32,128]{3,2,1,0:T(8,128)}, u32[]{:S(2)}) copy-start(f32[64,4,32,128]{3,2,1,0:T(8,128)} %fields.3) | copy-start | bytes 12582916
  1.7 6.7 %collective-permute-start = (f32[64,4,1,128]{3,2,1,0:T(1,128)S(1)}, f32[64,4,1,128]{3,2,1,0:T(1,128)S(1)}, u32[]{:S(2)}, u32[]{:S(2)}) collective-permute-start(f32[64,4,1,128]{3,2,1,0:T(1,128)S(1)} %get-tuple-element.26), channel_id=1, source_target_pairs={{0,1},{2,3},{4,5},{6,7},{1,0},{3,2},{5,4},{7,6},{8,9},{10,11},{12,... | collective-permute-start | bytes 393224 | tf_op jit(solution)/shard_map/ppermute | solution.py:343
  1.8 6.6 %collective-permute-start.1 = (f32[64,4,1,128]{3,2,1,0:T(1,128)S(1)}, f32[64,4,1,128]{3,2,1,0:T(1,128)S(1)}, u32[]{:S(2)}, u32[]{:S(2)}) collective-permute-start(f32[64,4,1,128]{3,2,1,0:T(1,128)S(1)} %get-tuple-element.27), channel_id=1, source_target_pairs={{1,2},{3,4},{5,6},{7,0},{2,1},{4,3},{6,5},{0,7},{9,10},{11,12},{13... | collective-permute-start | bytes 393224 | tf_op jit(solution)/shard_map/ppermute | solution.py:341
  4.2 4.3 %collective-permute-start.2 = (f32[4,32,128]{2,1,0:T(8,128)S(1)}, f32[4,32,128]{2,1,0:T(8,128)S(1)}, u32[]{:S(2)}, u32[]{:S(2)}) collective-permute-start(f32[4,32,128]{2,1,0:T(8,128)S(1)} %get-tuple-element.28), channel_id=1, source_target_pairs={{0,8},{16,24},{32,40},{48,56},{64,72},{80,88},{96,104},{112,120},{... | collective-permute-start | bytes 196616 | tf_op jit(solution)/shard_map/ppermute | solution.py:342
